TPU v7x, 512 devices: a whole 4x8x8 slice. The times are simulated.
512 devices in a mesh: row: 32 (over y, x_hi, core), col: 16 (over x_lo, z).
Axes of the slice: x: 4 (x_hi: 2, x_lo: 2; x = x_hi * 2 + x_lo), y: 8, z: 8, core: 2. Of those that a mesh axis runs over, the one named last changes fastest.
Arguments:
- positions: int32 [32, 16, 2, 2], P('row', 'col'), may hold values from 0 to 255, as said below
- measured: bfloat16 [32, 16, 2, 256, 256], P('row', 'col'), may hold values from 0.099609375 to 3
- object_field: float32 [2, 8192, 4096], P(None, 'row', 'col'), may hold values from -5 to 5
- probe: float32 [2, 256, 256], replicated, may hold values from -5 to 5
Outputs:
- new_object: float32 [2, 8192, 4096], P(None, 'row', 'col')
- new_probe: float32 [2, 256, 256], replicated
Inputs may be any that keep to these rules, and one draw needn't show every extreme that they name: `positions`: row offsets lie below 256 and column offsets below 256; the first position of the first tile sits at (255, 255) and the last position of the last tile at (0, 0).
All inputs are finite; a program needn't handle non-finite values.
Results may differ from a plain program's by a relative error of at most 0.0003.
Values sent between devices are 32-bit elements; how exact they have to be, the bound alone decides.
No kernel may reach another device: no remote copies, remote signals or barrier semaphores. Data moves between devices by JAX's collectives and lax.ppermute only.
A program may use at most 192 MiB of HBM per device.

v0:
```python
import math

import jax
import jax.numpy as jnp
from jax import lax
from jax.sharding import PartitionSpec as P

highest = lax.Precision.HIGHEST


def passed_along(value, axis, steps):
    count = lax.axis_size(axis)
    leading, last = (max(0, -steps), min(count, count - steps))
    return lax.ppermute(value, axis, [(source, source + steps) for source in range(leading, last)])


def dft_tables(length):
    indices = jnp.arange(length, dtype=jnp.int32)
    phases = indices[:, None] * indices[None, :] % length
    angles = phases.astype(jnp.float32) * (2.0 * math.pi / length)
    factor = 1.0 / math.sqrt(length)
    return (jnp.cos(angles) * factor, jnp.sin(angles) * factor)


def matmul(left, right):
    return jnp.dot(left, right, precision=highest, preferred_element_type=jnp.float32)


def forward(real_part, imag_part, cosine, sine_table):
    left_real = matmul(cosine, real_part) + matmul(sine_table, imag_part)
    left_imag = matmul(cosine, imag_part) - matmul(sine_table, real_part)
    return (
        matmul(left_real, cosine) + matmul(left_imag, sine_table),
        matmul(left_imag, cosine) - matmul(left_real, sine_table),
    )


def backward(real_part, imag_part, cosine, sine_table):
    left_real = matmul(cosine, real_part) - matmul(sine_table, imag_part)
    left_imag = matmul(cosine, imag_part) + matmul(sine_table, real_part)
    return (
        matmul(left_real, cosine) - matmul(left_imag, sine_table),
        matmul(left_imag, cosine) + matmul(left_real, sine_table),
    )


def window_terms(window, probe, offsets, amplitude):
    side = probe.shape[1]
    zero = jnp.zeros((), jnp.int32)
    probe_real = probe[0]
    probe_imag = probe[1]
    cosine, sine_table = dft_tables(side)
    lighting = probe_real * probe_real + probe_imag * probe_imag
    layers = 3

    def visit(member, carry):
        canvas, numerator, weight = carry
        spot = offsets[member]
        patch = lax.dynamic_slice(window, (zero, spot[0], spot[1]), (2, side, side))
        patch_real = patch[0]
        patch_imag = patch[1]
        exit_real = probe_real * patch_real - probe_imag * patch_imag
        exit_imag = probe_real * patch_imag + probe_imag * patch_real
        far_real, far_imag = forward(exit_real, exit_imag, cosine, sine_table)
        modulus = jnp.sqrt(jnp.maximum(far_real * far_real + far_imag * far_imag, 0.25))
        ratio = amplitude[member] / modulus
        chi_real, chi_imag = backward(
            far_real * ratio - far_real, far_imag * ratio - far_imag, cosine, sine_table
        )
        object_real = probe_real * chi_real + probe_imag * chi_imag
        object_imag = probe_real * chi_imag - probe_imag * chi_real
        numerator = numerator + jnp.stack(
            [
                patch_real * chi_real + patch_imag * chi_imag,
                patch_real * chi_imag - patch_imag * chi_real,
            ]
        )
        weight = weight + patch_real * patch_real + patch_imag * patch_imag
        terms = jnp.stack([object_real, object_imag, lighting])
        current = lax.dynamic_slice(canvas, (zero, spot[0], spot[1]), (layers, side, side))
        canvas = lax.dynamic_update_slice(canvas, current + terms, (zero, spot[0], spot[1]))
        return (canvas, numerator, weight)

    start = (
        jnp.zeros((layers, window.shape[1], window.shape[2]), jnp.float32),
        jnp.zeros((2, side, side), jnp.float32),
        jnp.zeros((side, side), jnp.float32),
    )
    return lax.fori_loop(0, offsets.shape[0], visit, start)


def body(positions, measured, object_field, probe):
    offsets = positions[0, 0]
    amplitude = measured[0, 0]
    tile_rows = object_field.shape[1]
    tile_cols = object_field.shape[2]
    side = probe.shape[1]
    below_strip = passed_along(object_field, "row", -1)
    tall_block = jnp.concatenate([object_field, below_strip], 1)
    right_strip = passed_along(tall_block, "col", -1)
    window = jnp.concatenate([tall_block, right_strip], 2)
    gradient, numerator, weight = window_terms(window, probe, offsets, amplitude)
    incoming = passed_along(gradient[:, :, tile_cols:], "col", 1)
    gradient = gradient[:, :, :tile_cols].at[:, :, :side].add(incoming)
    arriving = passed_along(gradient[:, tile_rows:, :], "row", 1)
    gradient = gradient[:, :tile_rows, :].at[:, :side, :].add(arriving)
    object_step = gradient[:2]
    lit_tile = gradient[2]
    new_object = object_field + object_step / (lit_tile + 1.0)
    total_step, total_weight = lax.psum((numerator, weight), ("row", "col"))
    new_probe = probe + total_step / (total_weight + 1.0)
    return (new_object, new_probe)


def solution(mesh):
    in_specs = (
        P("row", "col", None, None),
        P("row", "col", None, None, None),
        P(None, "row", "col"),
        P(),
    )
    out_specs = (P(None, "row", "col"), P())
    return jax.shard_map(body, mesh=mesh, in_specs=in_specs, out_specs=out_specs, check_vma=False)
```

profile of v0, /device:TPU:1, one launch (start us, length us, event | category | flops | bytes accessed | tf_op | source)
XLA Modules:
  0.0 444.1 jit_solution(13301558798026533096)
XLA Ops:
  7.2 8.9 %collective-permute-start = (f32[2,256,256]{2,1,0:T(8,128)}, f32[2,256,256]{2,1,0:T(8,128)S(1)}, u32[]{:S(2)}, u32[]{:S(2)}) collective-permute-start(f32[2,256,256]{2,1,0:T(8,128)} %param.16), channel_id=1, source_target_pairs={{16,0},{32,16},{48,32},{64,48},{80,64},{96,80},{112,96},{128,112},... | collective-permute-start | bytes 1572872 | tf_op jit(solution)/shard_map/ppermute | solution.py:14
  17.2 3.2 collective-permute-done
  22.6 23.0 %collective-permute-done.1 = f32[2,512,256]{2,1,0:T(8,128)} collective-permute-done((f32[2,512,256]{2,1,0:T(8,128)S(1)}, f32[2,512,256]{2,1,0:T(8,128)}, u32[]{:S(2)}, u32[]{:S(2)}) %collective-permute-start.1) | collective-permute-done | bytes 1048608 | tf_op jit(solution)/shard_map/ppermute | solution.py:14
  45.6 1.8 pad_maximum_fusion
  47.5 2.0 broadcast_in_dim.6
  49.5 90.8 %while.23 = (s32[]{:T(128)}, f32[3,512,512]{2,1,0:T(8,128)}, f32[2,256,256]{2,1,0:T(8,128)}, f32[256,256]{1,0:T(8,128)}, s32[2,2]{1,0:T(2,128)S(1)}, /*index=5*/...) while((s32[]{:T(128)}, f32[3,512,512]{2,1,0:T(8,128)}, ...), condition=%wide.region_1.2_spmd.clone.clone, body=%wide.region_0.1_spmd.clone.clone.sunk | while | flops 3242065920 | bytes 21758272 | solution.py:89
  55.6 1.5 convolution_subtract_fusion.7
  58.5 1.5 convolution_add_fusion.8
  65.9 2.5 fusion.154
  68.4 2.5 convolution_subtract_fusion.9
  72.3 2.5 fusion.152
  74.8 2.5 convolution_add_fusion.10
  80.2 2.3 add_bitcast_fusion.3
  82.5 1.7 maximum_add_fusion.4
  85.1 8.7 %dynamic_update_slice.10 = f32[3,512,512]{2,1,0:T(8,128)} dynamic-update-slice(f32[3,512,512]{2,1,0:T(8,128)} %get-tuple-element.497, f32[3,256,256]{2,1,0:T(8,128)S(1)} %maximum_add_fusion.4, s32[]{:T(128)} %constant.119.clone.1..sunk, s32[]{:T(128)S(6)} %select_n.135, s32[]{:T(128)S(6)} %select_n.136) | dynamic-update-slice | bytes 1572868 | tf_op jit(solution)/shard_map/while/body/eval_jaxpr/dynamic_update_slice | solution.py:81
  99.9 1.5 convolution_subtract_fusion.7
  102.8 1.5 convolution_add_fusion.8
  110.2 2.5 fusion.154
  112.7 2.5 convolution_subtract_fusion.9
  116.6 2.5 fusion.152
  119.1 2.5 convolution_add_fusion.10
  124.5 3.3 add_bitcast_fusion.3
  127.8 1.7 maximum_add_fusion.4
  129.5 1.9 maximum_add_fusion.5
  131.4 8.9 %dynamic_update_slice.10 = f32[3,512,512]{2,1,0:T(8,128)} dynamic-update-slice(f32[3,512,512]{2,1,0:T(8,128)} %get-tuple-element.497, f32[3,256,256]{2,1,0:T(8,128)S(1)} %maximum_add_fusion.4, s32[]{:T(128)} %constant.119.clone.1..sunk, s32[]{:T(128)S(6)} %select_n.135, s32[]{:T(128)S(6)} %select_n.136) | dynamic-update-slice | bytes 1572868 | tf_op jit(solution)/shard_map/while/body/eval_jaxpr/dynamic_update_slice | solution.py:81
  140.3 2.9 slice.99
  143.2 3.0 collective-permute-start.2
  146.2 32.3 %collective-permute-done.2 = f32[3,512,256]{2,1,0:T(8,128)} collective-permute-done((f32[3,512,256]{2,1,0:T(8,128)}, f32[3,512,256]{2,1,0:T(8,128)}, u32[]{:S(2)}, u32[]{:S(2)}) %collective-permute-start.2) | collective-permute-done | bytes 1572896 | tf_op jit(solution)/shard_map/ppermute | solution.py:14
  178.5 1.7 slice_add_fusion
  181.5 5.7 %collective-permute-start.3 = (f32[3,256,256]{2,1,0:T(8,128)S(1)}, f32[3,256,256]{2,1,0:T(8,128)}, u32[]{:S(2)}, u32[]{:S(2)}) collective-permute-start(f32[3,256,256]{2,1,0:T(8,128)S(1)} %slice.113), channel_id=1, source_target_pairs={{0,16},{16,32},{32,48},{48,64},{64,80},{80,96},{96,112},{112,128},... | collective-permute-start | bytes 2359304 | tf_op jit(solution)/shard_map/ppermute | solution.py:14
  187.1 245.0 %all-reduce.3.cloned.1.call-done = (f32[2,256,256]{2,1,0:T(8,128)}, f32[256,256]{1,0:T(8,128)}) async-done(((f32[2,256,256]{2,1,0:T(8,128)}, f32[256,256]{1,0:T(8,128)}), (f32[2,256,256]{2,1,0:T(8,128)}, f32[256,256]{1,0:T(8,128)})) %all-reduce.3.cloned.1.call-update) | async-done | bytes 786448 | tf_op jit(solution)/shard_map/psum | solution.py:110
  433.1 2.0 divide_add_fusion
  (56 shorter events, 36.6 us)
Async XLA Ops:
  7.2 14.7 %copy-start.3 = (f32[2,256,256]{2,1,0:T(8,128)S(1)}, f32[2,256,256]{2,1,0:T(8,128)}, u32[]{:S(2)}) copy-start(f32[2,256,256]{2,1,0:T(8,128)} %param.17) | copy-start | bytes 1572868
  7.2 425.0 %all-reduce.3.cloned.1.call-start = ((), (), s32[]{:S(2)}) async-start(), calls=%async_computation | async-start | bytes 1572864 | tf_op jit(solution)/shard_map/psum | solution.py:110
  7.2 13.2 %collective-permute-start = (f32[2,256,256]{2,1,0:T(8,128)}, f32[2,256,256]{2,1,0:T(8,128)S(1)}, u32[]{:S(2)}, u32[]{:S(2)}) collective-permute-start(f32[2,256,256]{2,1,0:T(8,128)} %param.16), channel_id=1, source_target_pairs={{16,0},{32,16},{48,32},{64,48},{80,64},{96,80},{112,96},{128,112},... | collective-permute-start | bytes 1572872 | tf_op jit(solution)/shard_map/ppermute | solution.py:14
  20.5 2.1 copy-start.5
  20.5 25.1 %collective-permute-start.1 = (f32[2,512,256]{2,1,0:T(8,128)S(1)}, f32[2,512,256]{2,1,0:T(8,128)}, u32[]{:S(2)}, u32[]{:S(2)}) collective-permute-start(f32[2,512,256]{2,1,0:T(8,128)S(1)} %constant_dynamic-update-slice_fusion), channel_id=1, source_target_pairs={{1,0},{2,1},{3,2},{4,3},{5,4},{6,5},{7,6},{8,7},{9,8},{10,9},{11,1... | collective-permute-start | bytes 3145736 | tf_op jit(solution)/shard_map/ppermute | solution.py:14
  47.4 2.1 copy-start.7
  140.3 38.2 %copy-start = (f32[3,512,512]{2,1,0:T(8,128)S(1)}, f32[3,512,512]{2,1,0:T(8,128)}, u32[]{:S(2)}) copy-start(f32[3,512,512]{2,1,0:T(8,128)} %get-tuple-element.285) | copy-start | bytes 9437188
  143.2 35.3 %collective-permute-start.2 = (f32[3,512,256]{2,1,0:T(8,128)}, f32[3,512,256]{2,1,0:T(8,128)}, u32[]{:S(2)}, u32[]{:S(2)}) collective-permute-start(f32[3,512,256]{2,1,0:T(8,128)} %slice.99), channel_id=1, source_target_pairs={{0,1},{1,2},{2,3},{3,4},{4,5},{5,6},{6,7},{7,8},{8,9},{9,10},{10,1... | collective-permute-start | bytes 4718600 | tf_op jit(solution)/shard_map/ppermute | solution.py:14
  180.2 1.2 copy-start.1
  181.4 251.7 %copy-start.4 = (f32[2,256,256]{2,1,0:T(8,128)S(1)}, f32[2,256,256]{2,1,0:T(8,128)}, u32[]{:S(2)}) copy-start(f32[2,256,256]{2,1,0:T(8,128)} %param.17) | copy-start | bytes 1572868
  181.4 253.7 %copy-start.2 = (f32[3,512,256]{2,1,0:T(8,128)S(1)}, f32[3,512,256]{2,1,0:T(8,128)}, u32[]{:S(2)}) copy-start(f32[3,512,256]{2,1,0:T(8,128)} %copy-done.1) | copy-start | bytes 4718596
  181.5 253.7 %collective-permute-start.3 = (f32[3,256,256]{2,1,0:T(8,128)S(1)}, f32[3,256,256]{2,1,0:T(8,128)}, u32[]{:S(2)}, u32[]{:S(2)}) collective-permute-start(f32[3,256,256]{2,1,0:T(8,128)S(1)} %slice.113), channel_id=1, source_target_pairs={{0,16},{16,32},{32,48},{48,64},{64,80},{80,96},{96,112},{112,128},... | collective-permute-start | bytes 2359304 | tf_op jit(solution)/shard_map/ppermute | solution.py:14
  433.1 3.3 copy-start.6
Sparse Core Ops, SparseCore 0:
  146.4 285.7 all-reduce.2
where the time goes:
time: 446 us; the launch traced here: 444 us
  waiting for transfers between devices  304 us (68%)
  matrix products  57.6 us (13%)
  local copies, waits for them, and re-layouts  26.3 us (6%)
  starting transfers between devices  19 us (4%)
  other arithmetic  15.9 us (4%)
  between operations  14.2 us (3%)
  loops' own time  7.65 us (2%)
    psum x1, waiting for transfers between devices, body(): total_step, total_weight = lax.psum((numerator, weight), ('row', 'col'))  245 us
    ppermute x4, waiting for transfers between devices, passed_along(): lax.ppermute(value, axis, [(source, source + steps) for source in range(l...  58.5 us
    dot_general x32, matrix products, matmul(): jnp.dot(left, right, precision=highest, preferred_element_type=jnp.float32)  57.6 us
    ppermute x4, starting transfers between devices, passed_along(): lax.ppermute(value, axis, [(source, source + steps) for source in range(l...  18.9 us
    dynamic_update_slice x2, local copies, waits for them, and re-layouts, visit(): lax.dynamic_update_slice(canvas, current + terms, (zero, spot[0], spot[1]))  17.7 us
  transfers between devices with their start and end apart: 5, of which 4 were waited for; matrix products, arithmetic and copies ran while one was open for 1% of the time, Pallas kernels for 0%

commit v1 on v0

v1 whole, which is shorter than its diff:
```python
import functools
import math

import jax
import jax.numpy as jnp
import ml_dtypes
import numpy as np
from jax import lax
from jax.experimental import pallas as pl
from jax.experimental.pallas import tpu as pltpu
from jax.sharding import Mesh
from jax.sharding import PartitionSpec as P

SIDE = 256
ROW = ("y", "xh", "c")
COL = ("xl", "z")
PLANE = ("y", "xh", "xl")


def passed_along(value, axis, steps):
    count = lax.axis_size(axis)
    leading, last = (max(0, -steps), min(count, count - steps))
    return lax.ppermute(value, axis, [(source, source + steps) for source in range(leading, last)])


def dft_tables():
    indices = np.arange(SIDE)
    angles = (indices[:, None] * indices[None, :] % SIDE) * (2.0 * math.pi / SIDE)
    cosine = np.cos(angles) / math.sqrt(SIDE)
    sine = np.sin(angles) / math.sqrt(SIDE)
    forward = np.block([[cosine, sine], [-sine, cosine]])
    both = np.stack([forward, forward.T])
    head = both.astype(ml_dtypes.bfloat16)
    rest = (both - head.astype(np.float64)).astype(ml_dtypes.bfloat16)
    return np.stack([head, rest], 1)


def halves(value):
    head = value.astype(jnp.bfloat16)
    return head, (value - head.astype(jnp.float32)).astype(jnp.bfloat16)


def dot(left, right):
    return jnp.dot(left, right, preferred_element_type=jnp.float32)


def apply_left(tables, which, value):
    head, rest = halves(value)
    return dot(tables[which, 0], head) + dot(tables[which, 0], rest) + dot(tables[which, 1], head)


def apply_right(tables, which, value):
    head, rest = halves(value)
    return dot(head, tables[which, 0]) + dot(rest, tables[which, 0]) + dot(head, tables[which, 1])


def rolled(value, rows, cols):
    return pltpu.roll(pltpu.roll(value, rows, 0), cols, 1)


def quadrants(row, col):
    below = lax.broadcasted_iota(jnp.int32, (SIDE, SIDE), 0) < row
    right = lax.broadcasted_iota(jnp.int32, (SIDE, SIDE), 1) < col
    return below, right


def prepare_kernel(own, left, upper, corner, probe, rolled_probe, lighting):
    total = jnp.ones((SIDE, SIDE), jnp.float32)
    for k in range(2):
        row, col = own[k, 0], own[k, 1]
        real = rolled(probe[0], row, col)
        imag = rolled(probe[1], row, col)
        rolled_probe[k, 0] = real
        rolled_probe[k, 1] = imag
        below, right = quadrants(row, col)
        total += jnp.where(below | right, 0.0, real * real + imag * imag)
    intensity = probe[0] * probe[0] + probe[1] * probe[1]
    for k in range(2):
        for spots, lies_below, lies_right in ((left, False, True), (upper, True, False), (corner, True, True)):
            row, col = spots[k, 0], spots[k, 1]
            below, right = quadrants(row, col)
            inside = (below == lies_below) & (right == lies_right)
            total += jnp.where(inside, rolled(intensity, row, col), 0.0)
    lighting[...] = total


def visit_kernel(
    own, core, tile, right_tile, below_tile, corner_tile, rolled_probe, amplitude, tables,
    step_own, step_right, step_row, kept, sent, patches,
):
    exits = []
    for k in range(2):
        below, right = quadrants(own[k, 0], own[k, 1])
        for part in range(2):
            patches[k, part] = jnp.where(
                below,
                jnp.where(right, corner_tile[part], below_tile[part]),
                jnp.where(right, right_tile[part], tile[part]),
            )
        pr, pi = rolled_probe[k, 0], rolled_probe[k, 1]
        qr, qi = patches[k, 0], patches[k, 1]
        exits.append(jnp.concatenate([pr * qr - pi * qi, pr * qi + pi * qr], 0))
    field = apply_left(tables, 0, jnp.concatenate(exits, 1))
    field = jnp.concatenate(
        [jnp.concatenate([field[:SIDE, k * SIDE : (k + 1) * SIDE], field[SIDE:, k * SIDE : (k + 1) * SIDE]], 1) for k in range(2)], 0
    )
    far = apply_right(tables, 1, field)
    far_real, far_imag = far[:, :SIDE], far[:, SIDE:]
    power = jnp.maximum(far_real * far_real + far_imag * far_imag, 0.25)
    factor = amplitude[...].reshape(2 * SIDE, SIDE).astype(jnp.float32) * lax.rsqrt(power) - 1.0
    change_real, change_imag = far_real * factor, far_imag * factor
    change = jnp.concatenate(
        [jnp.concatenate([change_real[k * SIDE : (k + 1) * SIDE], change_imag[k * SIDE : (k + 1) * SIDE]], 0) for k in range(2)], 1
    )
    field = apply_left(tables, 1, change)
    field = jnp.concatenate(
        [jnp.concatenate([field[:SIDE, k * SIDE : (k + 1) * SIDE], field[SIDE:, k * SIDE : (k + 1) * SIDE]], 1) for k in range(2)], 0
    )
    chi = apply_right(tables, 0, field)
    numerator = [jnp.zeros((SIDE, SIDE), jnp.float32)] * 3
    steps = [[jnp.zeros((SIDE, SIDE), jnp.float32)] * 4 for _ in range(2)]
    for k in range(2):
        row, col = own[k, 0], own[k, 1]
        below, right = quadrants(row, col)
        chi_real = chi[k * SIDE : (k + 1) * SIDE, :SIDE]
        chi_imag = chi[k * SIDE : (k + 1) * SIDE, SIDE:]
        pr, pi = rolled_probe[k, 0], rolled_probe[k, 1]
        qr, qi = patches[k, 0], patches[k, 1]
        back_row, back_col = (SIDE - row) & (SIDE - 1), (SIDE - col) & (SIDE - 1)
        terms = (qr * chi_real + qi * chi_imag, qr * chi_imag - qi * chi_real, qr * qr + qi * qi)
        numerator = [total + rolled(term, back_row, back_col) for total, term in zip(numerator, terms)]
        places = (
            jnp.logical_not(below | right),
            right & jnp.logical_not(below),
            below & jnp.logical_not(right),
            below & right,
        )
        for part, term in enumerate((pr * chi_real + pi * chi_imag, pr * chi_imag - pi * chi_real)):
            steps[part] = [total + jnp.where(place, term, 0.0) for total, place in zip(steps[part], places)]
    for part in range(2):
        step_own[part] = steps[part][0]
        step_right[part] = steps[part][1]
        step_row[0, part] = steps[part][2]
        step_row[1, part] = steps[part][3]
    first = core[0] == 0
    half = SIDE // 2
    for layer in range(3):
        one, other = numerator[layer][:, :half], numerator[layer][:, half:]
        kept[:, layer] = jnp.where(first, one, other).reshape(SIDE // 8, 8, half)
        sent[:, layer] = jnp.where(first, other, one).reshape(SIDE // 8, 8, half)


def vmem():
    return pl.BlockSpec(memory_space=pltpu.VMEM)


def smem():
    return pl.BlockSpec(memory_space=pltpu.SMEM)


def shape(*sizes):
    return jax.ShapeDtypeStruct(sizes, jnp.float32)


def prepare(own, left, upper, corner, probe):
    return pl.pallas_call(
        prepare_kernel,
        out_shape=(shape(2, 2, SIDE, SIDE), shape(SIDE, SIDE)),
        in_specs=[smem()] * 4 + [vmem()],
        out_specs=(vmem(), vmem()),
        cost_estimate=pl.CostEstimate(flops=4000000, bytes_accessed=4 << 20, transcendentals=0),
        compiler_params=pltpu.CompilerParams(vmem_limit_bytes=16 << 20),
    )(own, left, upper, corner, probe)


def visit(own, core, tile, right_tile, below_tile, corner_tile, rolled_probe, amplitude, tables):
    rows = SIDE // 8
    return pl.pallas_call(
        visit_kernel,
        out_shape=(
            shape(2, SIDE, SIDE),
            shape(2, SIDE, SIDE),
            shape(2, 2, SIDE, SIDE),
            shape(rows, 3, 8, SIDE // 2),
            shape(rows, 3, 8, SIDE // 2),
        ),
        in_specs=[smem(), smem()] + [vmem()] * 7,
        out_specs=(vmem(),) * 5,
        scratch_shapes=[pltpu.VMEM((2, 2, SIDE, SIDE), jnp.float32)],
        cost_estimate=pl.CostEstimate(flops=24 * 2 * 256**3 * 4, bytes_accessed=8 << 20, transcendentals=131072),
        compiler_params=pltpu.CompilerParams(vmem_limit_bytes=32 << 20),
    )(own, core, tile, right_tile, below_tile, corner_tile, rolled_probe, amplitude, tables)


def everywhere(value, axis):
    copies = jnp.broadcast_to(value[None], (lax.axis_size(axis),) + value.shape)
    return lax.all_to_all(copies, axis, 0, 0)


def body(positions, measured, object_field, probe):
    own = positions[0, 0]
    amplitude = measured[0, 0]
    right_tile = passed_along(object_field, COL, -1)
    below_tile = passed_along(object_field, ROW, -1)
    left = passed_along(own, COL, 1)
    upper = passed_along(own, ROW, 1)
    corner = passed_along(left, ROW, 1)
    corner_tile = passed_along(right_tile, ROW, -1)
    rolled_probe, lighting = prepare(own, left, upper, corner, probe)
    core = lax.axis_index("c")
    step_own, step_right, step_row, kept, sent = visit(
        own, core[None], object_field, right_tile, below_tile, corner_tile, rolled_probe, amplitude, jnp.asarray(dft_tables())
    )
    other = lax.ppermute(sent, "c", [(0, 1), (1, 0)])
    step_row = passed_along(step_row, ROW, 1)
    rows = SIDE // 8
    summed = lax.all_to_all((kept + other).reshape(rows, 24, SIDE // 2), PLANE, 0, 0).sum(0)
    step_right = passed_along(step_right + step_row[1], COL, 1)
    summed = everywhere(summed, "z").sum(0).reshape(3, 8, SIDE // 2)
    place = lax.axis_index(PLANE)
    mine = lax.dynamic_slice(probe, (0, place * 8, core * (SIDE // 2)), (2, 8, SIDE // 2))
    mine = mine + summed[:2] / (summed[2] + 1.0)
    near = everywhere(mine.reshape(16, SIDE // 2), PLANE)
    far = lax.ppermute(near, "c", [(0, 1), (1, 0)])
    pair = jnp.where(core == 0, jnp.stack([near, far]), jnp.stack([far, near]))
    new_probe = pair.reshape(2, rows, 2, 8, SIDE // 2).transpose(2, 1, 3, 0, 4).reshape(2, SIDE, SIDE)
    new_object = object_field + (step_own + step_row[0] + step_right) / lighting
    return (new_object, new_probe)


def solution(mesh):
    split = Mesh(mesh.devices.reshape(8, 2, 2, 2, 8), ROW + COL)
    in_specs = (P(ROW, COL), P(ROW, COL), P(None, ROW, COL), P())
    out_specs = (P(None, ROW, COL), P())
    return jax.shard_map(body, mesh=split, in_specs=in_specs, out_specs=out_specs, check_vma=False)
```

time: 446 us -> 132 us (0.30)
  waiting for transfers between devices: 304 us -> 31.1 us
  starting transfers between devices: 19 us -> 76.9 us
  matrix products: 57.6 us -> 0 us
  local copies, waits for them, and re-layouts: 26.3 us -> 9.19 us
  between operations: 14.2 us -> 0.86 us
  other arithmetic: 15.9 us -> 5.48 us
  Pallas kernels: 0 us -> 7.81 us
  loops' own time: 7.65 us -> 0 us
    psum x1 -> x0, waiting for transfers between devices: 245 us -> none  [body(): total_step, total_weight = lax.psum((numerator, weight), ('row', 'col'))]
    dot_general x32 -> x0, matrix products: 57.6 us -> none  [matmul(): jnp.dot(left, right, precision=highest, preferred_element_type=jnp.float32)]
    ppermute x4 -> x8, waiting for transfers between devices: 58.5 us -> 2.41 us  [passed_along(): lax.ppermute(value, axis, [(source, source + steps) for source in range(l...]
    all_to_all x0 -> x3, starting transfers between devices: none -> 35.1 us  [the longest x1 23.3 us: body(): lax.all_to_all((kept + other).reshape(rows, 24, SIDE // 2), PLANE, 0, 0)]
    all_to_all x0 -> x3, waiting for transfers between devices: none -> 28.6 us  [the longest x1 14.4 us: body(): lax.all_to_all((kept + other).reshape(rows, 24, SIDE // 2), PLANE, 0, 0)]
    ppermute x4 -> x8, starting transfers between devices: 18.9 us -> 37.8 us  [passed_along(): lax.ppermute(value, axis, [(source, source + steps) for source in range(l...]
    dynamic_update_slice x2 -> x0, local copies, waits for them, and re-layouts: 17.7 us -> none  [visit(): lax.dynamic_update_slice(canvas, current + terms, (zero, spot[0], spot[1]))]
    add x12 -> x3, other arithmetic: 14 us -> 3.1 us  [the longest x1 1.99 us: body(): new_object = object_field + (step_own + step_row[0] + step_right) / lighting]
  transfers between devices with their start and end apart: 5 -> 13, of which waited for: 4 -> 5; matrix products, arithmetic and copies ran while one was open for 1% -> 5% of each run, Pallas kernels for 0% -> 1%
where the time goes in v1:
time: 132 us; the launch traced here: 131 us
  starting transfers between devices  76.9 us (58%)
  waiting for transfers between devices  31.1 us (24%)
  local copies, waits for them, and re-layouts  9.19 us (7%)
  Pallas kernels  7.81 us (6%)
  other arithmetic  5.48 us (4%)
    ppermute x8, starting transfers between devices, passed_along(): lax.ppermute(value, axis, [(source, source + steps) for source in range(l...  37.8 us
    all_to_all x1, starting transfers between devices, body(): lax.all_to_all((kept + other).reshape(rows, 24, SIDE // 2), PLANE, 0, 0)  23.3 us
    all_to_all x1, waiting for transfers between devices, body(): lax.all_to_all((kept + other).reshape(rows, 24, SIDE // 2), PLANE, 0, 0)  14.4 us
    all_to_all x2, waiting for transfers between devices, everywhere(): return lax.all_to_all(copies, axis, 0, 0)  14.3 us
    all_to_all x2, starting transfers between devices, everywhere(): return lax.all_to_all(copies, axis, 0, 0)  11.8 us
    unnamed x18, local copies, waits for them, and re-layouts  7.81 us
    pallas_call x1, Pallas kernels, visit(): pl.pallas_call(visit_kernel, out_shape=(shape(2, SIDE, SIDE), shape(2, SI...  5.93 us
  transfers between devices with their start and end apart: 13, of which 5 were waited for; matrix products, arithmetic and copies ran while one was open for 5% of the time, Pallas kernels for 1%

profile of v1, /device:TPU:1, one launch (start us, length us, event | category | flops | bytes accessed | tf_op | source)
XLA Modules:
  0.0 131.3 jit_solution(17032308389803958354)
XLA Ops:
  0.6 1.3 collective-permute-start
  1.9 8.8 %collective-permute-start.1 = (f32[2,256,256]{2,1,0:T(8,128)}, f32[2,256,256]{2,1,0:T(8,128)S(1)}, u32[]{:S(2)}, u32[]{:S(2)}) collective-permute-start(f32[2,256,256]{2,1,0:T(8,128)} %tile.1), channel_id=1, source_target_pairs={{16,0},{32,16},{48,32},{64,48},{80,64},{96,80},{112,96},{128,112},... | collective-permute-start | bytes 1572872 | tf_op jit(solution)/shard_map/ppermute | solution.py:23
  10.7 1.5 %collective-permute-done.right_tile = f32[2,256,256]{2,1,0:T(8,128)S(1)} collective-permute-done((f32[2,256,256]{2,1,0:T(8,128)}, f32[2,256,256]{2,1,0:T(8,128)S(1)}, u32[]{:S(2)}, u32[]{:S(2)}) %collective-permute-start) | collective-permute-done | bytes 524320 | tf_op jit(solution)/shard_map/ppermute | solution.py:23
  12.2 8.5 %collective-permute-start.2 = (f32[2,256,256]{2,1,0:T(8,128)S(1)}, f32[2,256,256]{2,1,0:T(8,128)S(1)}, u32[]{:S(2)}, u32[]{:S(2)}) collective-permute-start(f32[2,256,256]{2,1,0:T(8,128)S(1)} %collective-permute-done.right_tile), channel_id=1, source_target_pairs={{16,0},{32,16},{48,32},{64,48},{80,64},{96,80},{112,96},{128,112},... | collective-permute-start | bytes 1572872 | tf_op jit(solution)/shard_map/ppermute | solution.py:23
  20.7 3.7 %collective-permute-start.3 = (s32[2,2]{1,0:T(2,128)}, s32[2,2]{1,0:T(2,128)S(1)}, u32[]{:S(2)}, u32[]{:S(2)}) collective-permute-start(s32[2,2]{1,0:T(2,128)} %bitcast.36), channel_id=1, source_target_pairs={{0,1},{1,2},{2,3},{3,4},{4,5},{5,6},{6,7},{7,8},{8,9},{9,10},{10,1... | collective-permute-start | bytes 56 | tf_op jit(solution)/shard_map/ppermute | solution.py:23
  24.5 4.8 %collective-permute-start.4 = (s32[2,2]{1,0:T(2,128)}, s32[2,2]{1,0:T(2,128)S(1)}, u32[]{:S(2)}, u32[]{:S(2)}) collective-permute-start(s32[2,2]{1,0:T(2,128)} %bitcast.37), channel_id=1, source_target_pairs={{0,16},{16,32},{32,48},{48,64},{64,80},{80,96},{96,112},{112,128},... | collective-permute-start | bytes 56 | tf_op jit(solution)/shard_map/ppermute | solution.py:23
  29.3 2.1 %collective-permute-start.5 = (s32[2,2]{1,0:T(2,128)S(1)}, s32[2,2]{1,0:T(2,128)S(1)}, u32[]{:S(2)}, u32[]{:S(2)}) collective-permute-start(s32[2,2]{1,0:T(2,128)S(1)} %collective-permute-done.3.left), channel_id=1, source_target_pairs={{0,16},{16,32},{32,48},{48,64},{64,80},{80,96},{96,112},{112,128},... | collective-permute-start | bytes 56 | tf_op jit(solution)/shard_map/ppermute | solution.py:23
  31.5 0.9 collective-permute-done.5.corner
  32.3 1.0 copy-done
  34.1 1.9 %shard_map.68 = (f32[2,2,256,256]{3,2,1,0:T(8,128)S(1)}, f32[256,256]{1,0:T(8,128)S(1)}) custom-call(s32[2,2]{1,0:T(2,128)S(1)} %bitcast.38, s32[2,2]{1,0:T(2,128)S(1)} %collective-permute-done.3.left, s32[2,2]{1,0:T(2,128)S(1)} %collective-permute-done.4.upper, s32[2,2]{1,0:T(2,128)S(1)} %collective-permute-done.5.corner, f32[2,256,256]{2,1,0:T(8,128)S(1)} %copy-done), custom_call_target="tpu_custom_call" | custom-call | flops 4000000 | bytes 4194304 | tf_op jit(solution)/shard_map/pallas_call | solution.py:166
  36.0 0.8 copy-done.5
  36.8 1.0 copy-done.1
  38.5 1.0 copy-done.6
  39.5 0.9 copy-done.7
  40.5 1.6 %copy-done.8 = bf16[2,2,512,512]{3,2,1,0:T(8,128)(2,1)S(1)} copy-done((bf16[2,2,512,512]{3,2,1,0:T(8,128)(2,1)S(1)}, bf16[2,2,512,512]{3,2,1,0:T(8,128)(2,1)}, u32[]{:S(2)}) %copy-start.8) | copy-done | bytes 2097176
  42.1 5.9 %shard_map.69 = (f32[2,256,256]{2,1,0:T(8,128)S(1)}, f32[2,256,256]{2,1,0:T(8,128)S(1)}, f32[2,2,256,256]{3,2,1,0:T(8,128)S(1)}, f32[32,3,8,128]{3,2,1,0:T(8,128)S(1)}, f32[32,3,8,128]{3,2,1,0:T(8,128)S(1)}) custom-call(s32[2,2]{1,0:T(2,128)S(1)} %bitcast.39, s32[1]{0:T(128)} %bitcast.1.core, f32[2,256,256]{2,1,0:T(8,128)S(1)} %copy-done.1, ...), custom_call_target="tpu_custom_call" | custom-call | flops 3221225472 | bytes 8388608 | tf_op jit(solution)/shard_map/pallas_call | solution.py:178
  48.0 2.1 %collective-permute-start.8 = (f32[32,3,8,128]{3,2,1,0:T(8,128)S(1)}, f32[32,3,8,128]{3,2,1,0:T(8,128)S(1)}, u32[]{:S(2)}, u32[]{:S(2)}) collective-permute-start(f32[32,3,8,128]{3,2,1,0:T(8,128)S(1)} %get-tuple-element.15), channel_id=1, source_target_pairs={{0,16},{16,0},{1,17},{17,1},{2,18},{18,2},{3,19},{19,3},{4,20},{20... | collective-permute-start | bytes 1179656 | tf_op jit(solution)/shard_map/ppermute | solution.py:214
  50.1 5.3 %collective-permute-start.6 = (f32[2,2,256,256]{3,2,1,0:T(8,128)S(1)}, f32[2,2,256,256]{3,2,1,0:T(8,128)}, u32[]{:S(2)}, u32[]{:S(2)}) collective-permute-start(f32[2,2,256,256]{3,2,1,0:T(8,128)S(1)} %get-tuple-element.11), channel_id=1, source_target_pairs={{0,16},{16,32},{32,48},{48,64},{64,80},{80,96},{96,112},{112,128},... | collective-permute-start | bytes 3145736 | tf_op jit(solution)/shard_map/ppermute | solution.py:23
  55.4 0.8 add_bitcast_fusion
  56.2 23.3 %all-to-all-start = ((f32[32,24,128]{2,1,0:T(8,128)}), f32[32,24,128]{2,1,0:T(8,128)S(1)}, u32[]{:S(2)}, u32[]{:S(2)}) async-start(f32[32,24,128]{2,1,0:T(8,128)} %add_bitcast_fusion), calls=%async_computation | async-start | bytes 786432 | tf_op jit(solution)/shard_map/all_to_all | solution.py:217
  79.5 14.4 %all-to-all-done = f32[32,24,128]{2,1,0:T(8,128)S(1)} async-done(((f32[32,24,128]{2,1,0:T(8,128)}), f32[32,24,128]{2,1,0:T(8,128)S(1)}, u32[]{:S(2)}, u32[]{:S(2)}) %all-to-all-start) | async-done | bytes 393248 | tf_op jit(solution)/shard_map/all_to_all | solution.py:217
  94.6 3.4 %all-to-all-start.1 = ((f32[8,24,128]{2,1,0:T(8,128)}), f32[8,24,128]{2,1,0:T(8,128)S(1)}, u32[]{:S(2)}, u32[]{:S(2)}) async-start(f32[8,24,128]{2,1,0:T(8,128)} %broadcast_in_dim.9), calls=%async_computation.1 | async-start | bytes 196608 | tf_op jit(solution)/shard_map/all_to_all | solution.py:197
  98.0 1.1 fusion
  99.1 3.3 %collective-permute-start.7 = (f32[2,256,256]{2,1,0:T(8,128)S(1)}, f32[2,256,256]{2,1,0:T(8,128)S(1)}, u32[]{:S(2)}, u32[]{:S(2)}) collective-permute-start(f32[2,256,256]{2,1,0:T(8,128)S(1)} %fusion), channel_id=1, source_target_pairs={{0,1},{1,2},{2,3},{3,4},{4,5},{5,6},{6,7},{7,8},{8,9},{9,10},{10,1... | collective-permute-start | bytes 1572872 | tf_op jit(solution)/shard_map/ppermute | solution.py:23
  102.4 3.8 %all-to-all-done.1 = f32[8,24,128]{2,1,0:T(8,128)S(1)} async-done(((f32[8,24,128]{2,1,0:T(8,128)}), f32[8,24,128]{2,1,0:T(8,128)S(1)}, u32[]{:S(2)}, u32[]{:S(2)}) %all-to-all-start.1) | async-done | bytes 98336 | tf_op jit(solution)/shard_map/all_to_all | solution.py:197
  106.2 0.7 fusion.8
  106.9 0.7 broadcast_in_dim.21
  107.6 8.4 %all-to-all-start.2 = ((f32[32,16,128]{2,1,0:T(8,128)}), f32[32,16,128]{2,1,0:T(8,128)S(1)}, u32[]{:S(2)}, u32[]{:S(2)}) async-start(f32[32,16,128]{2,1,0:T(8,128)} %broadcast_in_dim.21), calls=%async_computation.2 | async-start | bytes 524288 | tf_op jit(solution)/shard_map/all_to_all | solution.py:197
  116.1 10.5 %all-to-all-done.2 = f32[32,16,128]{2,1,0:T(8,128)S(1)} async-done(((f32[32,16,128]{2,1,0:T(8,128)}), f32[32,16,128]{2,1,0:T(8,128)S(1)}, u32[]{:S(2)}, u32[]{:S(2)}) %all-to-all-start.2) | async-done | bytes 262176 | tf_op jit(solution)/shard_map/all_to_all | solution.py:197
  126.6 1.9 %collective-permute-start.9 = (f32[32,16,128]{2,1,0:T(8,128)S(1)}, f32[32,16,128]{2,1,0:T(8,128)S(1)}, u32[]{:S(2)}, u32[]{:S(2)}) collective-permute-start(f32[32,16,128]{2,1,0:T(8,128)S(1)} %all-to-all-done.2), channel_id=1, source_target_pairs={{0,16},{16,0},{1,17},{17,1},{2,18},{18,2},{3,19},{19,3},{4,20},{20... | collective-permute-start | bytes 786440 | tf_op jit(solution)/shard_map/ppermute | solution.py:224
  128.5 2.0 %fusion.4 = f32[2,256,256]{2,1,0:T(8,128)} fusion(f32[2,256,256]{2,1,0:T(8,128)S(1)} %copy-done.2, f32[2,256,256]{2,1,0:T(8,128)S(1)} %collective-permute-done.7, f32[2,256,256]{2,1,0:T(8,128)S(1)} %get-tuple-element.10, f32[2,2,256,256]{3,2,1,0:T(8,128)} %collective-permute-done.6, f32[256,256]{1,0:T(8,128)S(1)} %get-tuple-element.13), kind=kLoop, calls=%fused_computation.6 | loop fusion | flops 524288 | bytes 2883584 | tf_op jit(solution)/shard_map/add | solution.py:227
  130.5 0.8 copy_bitcast_fusion
  (24 shorter events, 2.1 us)
Async XLA Ops:
  0.6 11.6 %collective-permute-start = (f32[2,256,256]{2,1,0:T(8,128)}, f32[2,256,256]{2,1,0:T(8,128)S(1)}, u32[]{:S(2)}, u32[]{:S(2)}) collective-permute-start(f32[2,256,256]{2,1,0:T(8,128)} %tile.1), channel_id=1, source_target_pairs={{1,0},{2,1},{3,2},{4,3},{5,4},{6,5},{7,6},{8,7},{9,8},{10,9},{11,1... | collective-permute-start | bytes 1572872 | tf_op jit(solution)/shard_map/ppermute | solution.py:23
  1.9 34.0 %collective-permute-start.1 = (f32[2,256,256]{2,1,0:T(8,128)}, f32[2,256,256]{2,1,0:T(8,128)S(1)}, u32[]{:S(2)}, u32[]{:S(2)}) collective-permute-start(f32[2,256,256]{2,1,0:T(8,128)} %tile.1), channel_id=1, source_target_pairs={{16,0},{32,16},{48,32},{64,48},{80,64},{96,80},{112,96},{128,112},... | collective-permute-start | bytes 1572872 | tf_op jit(solution)/shard_map/ppermute | solution.py:23
  12.2 23.7 %collective-permute-start.2 = (f32[2,256,256]{2,1,0:T(8,128)S(1)}, f32[2,256,256]{2,1,0:T(8,128)S(1)}, u32[]{:S(2)}, u32[]{:S(2)}) collective-permute-start(f32[2,256,256]{2,1,0:T(8,128)S(1)} %collective-permute-done.right_tile), channel_id=1, source_target_pairs={{16,0},{32,16},{48,32},{64,48},{80,64},{96,80},{112,96},{128,112},... | collective-permute-start | bytes 1572872 | tf_op jit(solution)/shard_map/ppermute | solution.py:23
  20.7 8.6 %collective-permute-start.3 = (s32[2,2]{1,0:T(2,128)}, s32[2,2]{1,0:T(2,128)S(1)}, u32[]{:S(2)}, u32[]{:S(2)}) collective-permute-start(s32[2,2]{1,0:T(2,128)} %bitcast.36), channel_id=1, source_target_pairs={{0,1},{1,2},{2,3},{3,4},{4,5},{5,6},{6,7},{7,8},{8,9},{9,10},{10,1... | collective-permute-start | bytes 56 | tf_op jit(solution)/shard_map/ppermute | solution.py:23
  24.5 7.0 %collective-permute-start.4 = (s32[2,2]{1,0:T(2,128)}, s32[2,2]{1,0:T(2,128)S(1)}, u32[]{:S(2)}, u32[]{:S(2)}) collective-permute-start(s32[2,2]{1,0:T(2,128)} %bitcast.37), channel_id=1, source_target_pairs={{0,16},{16,32},{32,48},{48,64},{64,80},{80,96},{96,112},{112,128},... | collective-permute-start | bytes 56 | tf_op jit(solution)/shard_map/ppermute | solution.py:23
  29.3 3.0 %collective-permute-start.5 = (s32[2,2]{1,0:T(2,128)S(1)}, s32[2,2]{1,0:T(2,128)S(1)}, u32[]{:S(2)}, u32[]{:S(2)}) collective-permute-start(s32[2,2]{1,0:T(2,128)S(1)} %collective-permute-done.3.left), channel_id=1, source_target_pairs={{0,16},{16,32},{32,48},{48,64},{64,80},{80,96},{96,112},{112,128},... | collective-permute-start | bytes 56 | tf_op jit(solution)/shard_map/ppermute | solution.py:23
  32.3 1.0 copy-start
  33.4 0.7 copy-start.3
  36.0 0.8 copy-start.5
  36.8 1.0 copy-start.1
  37.8 0.7 copy-start.4
  38.5 1.0 copy-start.6
  39.5 0.9 copy-start.7
  40.5 1.6 %copy-start.8 = (bf16[2,2,512,512]{3,2,1,0:T(8,128)(2,1)S(1)}, bf16[2,2,512,512]{3,2,1,0:T(8,128)(2,1)}, u32[]{:S(2)}) copy-start(bf16[2,2,512,512]{3,2,1,0:T(8,128)(2,1)} %constant.37.clone.tables) | copy-start | bytes 6291460
  48.0 7.4 %collective-permute-start.8 = (f32[32,3,8,128]{3,2,1,0:T(8,128)S(1)}, f32[32,3,8,128]{3,2,1,0:T(8,128)S(1)}, u32[]{:S(2)}, u32[]{:S(2)}) collective-permute-start(f32[32,3,8,128]{3,2,1,0:T(8,128)S(1)} %get-tuple-element.15), channel_id=1, source_target_pairs={{0,16},{16,0},{1,17},{17,1},{2,18},{18,2},{3,19},{19,3},{4,20},{20... | collective-permute-start | bytes 1179656 | tf_op jit(solution)/shard_map/ppermute | solution.py:214
  50.1 47.9 %collective-permute-start.6 = (f32[2,2,256,256]{3,2,1,0:T(8,128)S(1)}, f32[2,2,256,256]{3,2,1,0:T(8,128)}, u32[]{:S(2)}, u32[]{:S(2)}) collective-permute-start(f32[2,2,256,256]{3,2,1,0:T(8,128)S(1)} %get-tuple-element.11), channel_id=1, source_target_pairs={{0,16},{16,32},{32,48},{48,64},{64,80},{80,96},{96,112},{112,128},... | collective-permute-start | bytes 3145736 | tf_op jit(solution)/shard_map/ppermute | solution.py:23
  56.2 72.3 %copy-start.2 = (f32[2,256,256]{2,1,0:T(8,128)S(1)}, f32[2,256,256]{2,1,0:T(8,128)}, u32[]{:S(2)}) copy-start(f32[2,256,256]{2,1,0:T(8,128)} %tile.1) | copy-start | bytes 1572868
  56.2 37.7 %all-to-all-start = ((f32[32,24,128]{2,1,0:T(8,128)}), f32[32,24,128]{2,1,0:T(8,128)S(1)}, u32[]{:S(2)}, u32[]{:S(2)}) async-start(f32[32,24,128]{2,1,0:T(8,128)} %add_bitcast_fusion), calls=%async_computation | async-start | bytes 786432 | tf_op jit(solution)/shard_map/all_to_all | solution.py:217
  94.6 11.6 %all-to-all-start.1 = ((f32[8,24,128]{2,1,0:T(8,128)}), f32[8,24,128]{2,1,0:T(8,128)S(1)}, u32[]{:S(2)}, u32[]{:S(2)}) async-start(f32[8,24,128]{2,1,0:T(8,128)} %broadcast_in_dim.9), calls=%async_computation.1 | async-start | bytes 196608 | tf_op jit(solution)/shard_map/all_to_all | solution.py:197
  99.1 29.4 %collective-permute-start.7 = (f32[2,256,256]{2,1,0:T(8,128)S(1)}, f32[2,256,256]{2,1,0:T(8,128)S(1)}, u32[]{:S(2)}, u32[]{:S(2)}) collective-permute-start(f32[2,256,256]{2,1,0:T(8,128)S(1)} %fusion), channel_id=1, source_target_pairs={{0,1},{1,2},{2,3},{3,4},{4,5},{5,6},{6,7},{7,8},{8,9},{9,10},{10,1... | collective-permute-start | bytes 1572872 | tf_op jit(solution)/shard_map/ppermute | solution.py:23
  107.6 19.0 %all-to-all-start.2 = ((f32[32,16,128]{2,1,0:T(8,128)}), f32[32,16,128]{2,1,0:T(8,128)S(1)}, u32[]{:S(2)}, u32[]{:S(2)}) async-start(f32[32,16,128]{2,1,0:T(8,128)} %broadcast_in_dim.21), calls=%async_computation.2 | async-start | bytes 524288 | tf_op jit(solution)/shard_map/all_to_all | solution.py:197
  126.6 3.9 %collective-permute-start.9 = (f32[32,16,128]{2,1,0:T(8,128)S(1)}, f32[32,16,128]{2,1,0:T(8,128)S(1)}, u32[]{:S(2)}, u32[]{:S(2)}) collective-permute-start(f32[32,16,128]{2,1,0:T(8,128)S(1)} %all-to-all-done.2), channel_id=1, source_target_pairs={{0,16},{16,0},{1,17},{17,1},{2,18},{18,2},{3,19},{19,3},{4,20},{20... | collective-permute-start | bytes 786440 | tf_op jit(solution)/shard_map/ppermute | solution.py:224

commit v2 on v1

v2 whole, which is shorter than its diff:
```python
import math

import jax
import jax.numpy as jnp
import ml_dtypes
import numpy as np
from jax import lax
from jax.experimental import pallas as pl
from jax.experimental.pallas import tpu as pltpu
from jax.sharding import Mesh
from jax.sharding import PartitionSpec as P

SIDE = 256
ROW = ("y", "xh", "c")
COL = ("xl", "z")
PLANE = ("xh", "xl", "z")


def passed_along(value, axis, steps):
    count = lax.axis_size(axis)
    leading, last = (max(0, -steps), min(count, count - steps))
    return lax.ppermute(value, axis, [(source, source + steps) for source in range(leading, last)])


def dft_tables():
    indices = np.arange(SIDE)
    angles = (indices[:, None] * indices[None, :] % SIDE) * (2.0 * math.pi / SIDE)
    cosine, sine = np.cos(angles) / math.sqrt(SIDE), np.sin(angles) / math.sqrt(SIDE)
    three = np.stack([cosine, sine, -sine])
    head = three.astype(ml_dtypes.bfloat16)
    rest = (three - head.astype(np.float64)).astype(ml_dtypes.bfloat16)
    return np.stack([head, rest], 1)


def halves(value):
    head = value.astype(jnp.bfloat16)
    return head, (value - head.astype(jnp.float32)).astype(jnp.bfloat16)


def dot(left, right):
    return jnp.dot(left, right, preferred_element_type=jnp.float32)


def block(tables, sign, which):
    up, down = (1, 2) if sign > 0 else (2, 1)
    upper = jnp.concatenate([tables[0, which], tables[up, which]], 1)
    return jnp.concatenate([upper, jnp.concatenate([tables[down, which], tables[0, which]], 1)], 0)


def apply_left(tables, sign, value):
    head, rest = halves(value)
    matrix = block(tables, sign, 0)
    return dot(matrix, head) + dot(matrix, rest) + dot(block(tables, sign, 1), head)


def apply_right(tables, sign, value):
    head, rest = halves(value)
    matrix = block(tables, sign, 0)
    return dot(head, matrix) + dot(rest, matrix) + dot(head, block(tables, sign, 1))


def to_columns(value):
    return jnp.concatenate(
        [jnp.concatenate([value[:SIDE, k * SIDE : (k + 1) * SIDE], value[SIDE:, k * SIDE : (k + 1) * SIDE]], 1) for k in range(2)], 0
    )


def rolled(value, rows, cols):
    return pltpu.roll(pltpu.roll(value, rows, 0), cols, 1)


def quadrants(row, col):
    below = lax.broadcasted_iota(jnp.int32, (SIDE, SIDE), 0) < row
    right = lax.broadcasted_iota(jnp.int32, (SIDE, SIDE), 1) < col
    return below, right


def prepare_kernel(own, probe, rolled_probe):
    for k in range(2):
        for part in range(2):
            rolled_probe[k, part] = rolled(probe[part], own[k, 0], own[k, 1])


def carried(block, first):
    line = lax.broadcasted_iota(jnp.int32, block.shape, 0)
    last = lax.broadcasted_iota(jnp.int32, block.shape, 1) == block.shape[1] - 1
    return [jnp.sum(jnp.where(last & (line == first + k), block, 0.0)).astype(jnp.int32) for k in range(4)]


def finish_kernel(own, probe, tile, step_own, step_row, step_right, new_tile):
    half = SIDE // 2
    intensity = probe[0] * probe[0] + probe[1] * probe[1]
    beside, above = step_right[0, :8, half:], step_row[1, 0, :8, half:]
    total = jnp.ones((SIDE, SIDE), jnp.float32)
    for spots, lies_below, lies_right in (
        ([own[k // 2, k % 2] for k in range(4)], False, False),
        (carried(beside, 4), False, True),
        (carried(above, 0), True, False),
        (carried(beside, 0), True, True),
    ):
        for k in range(2):
            row, col = spots[2 * k], spots[2 * k + 1]
            below, right = quadrants(row, col)
            inside = (below == lies_below) & (right == lies_right)
            total += jnp.where(inside, rolled(intensity, row, col), 0.0)
    last = lax.broadcasted_iota(jnp.int32, (SIDE, SIDE), 1) == SIDE - 1
    for part in range(2):
        arrived = step_row[0, part] + jnp.where(last, 0.0, step_right[part])
        new_tile[part] = tile[part] + (step_own[part] + arrived) / total


def visit_kernel(
    own, core, tile, right_real, right_imag, below_tile, corner_real, corner_imag, rolled_probe, amplitude,
    tables, kept, sent, step_own, step_right, step_row, patches, near_row, stored,
):
    right_tile, corner_tile = (right_real, right_imag), (corner_real, corner_imag)
    exits = []
    for k in range(2):
        below, right = quadrants(own[k, 0], own[k, 1])
        for part in range(2):
            patches[k, part] = jnp.where(
                below,
                jnp.where(right, corner_tile[part][...], below_tile[part]),
                jnp.where(right, right_tile[part][...], tile[part]),
            )
        pr, pi = rolled_probe[k, 0], rolled_probe[k, 1]
        qr, qi = patches[k, 0], patches[k, 1]
        exits.append(jnp.concatenate([pr * qr - pi * qi, pr * qi + pi * qr], 0))
    exits = jnp.concatenate(exits, 1)
    field = to_columns(apply_left(tables, 1, exits))
    far = apply_right(tables, -1, field)
    far_real, far_imag = far[:, :SIDE], far[:, SIDE:]
    power = jnp.maximum(far_real * far_real + far_imag * far_imag, 0.25)
    factor = amplitude[...].reshape(2 * SIDE, SIDE).astype(jnp.float32) * lax.rsqrt(power) - 1.0
    change_real, change_imag = far_real * factor, far_imag * factor
    change = jnp.concatenate(
        [jnp.concatenate([change_real[k * SIDE : (k + 1) * SIDE], change_imag[k * SIDE : (k + 1) * SIDE]], 0) for k in range(2)], 1
    )
    chi = apply_right(tables, 1, to_columns(apply_left(tables, -1, change)))
    numerator = [jnp.zeros((SIDE, SIDE), jnp.float32)] * 3
    for k in range(2):
        chi_real = chi[k * SIDE : (k + 1) * SIDE, :SIDE]
        chi_imag = chi[k * SIDE : (k + 1) * SIDE, SIDE:]
        qr, qi = patches[k, 0], patches[k, 1]
        back_row, back_col = (SIDE - own[k, 0]) & (SIDE - 1), (SIDE - own[k, 1]) & (SIDE - 1)
        terms = (qr * chi_real + qi * chi_imag, qr * chi_imag - qi * chi_real, qr * qr + qi * qi)
        numerator = [total + rolled(term, back_row, back_col) for total, term in zip(numerator, terms)]
    first = core[0] == 0
    half = SIDE // 2
    for layer in range(3):
        one, other = numerator[layer][:, :half], numerator[layer][:, half:]
        kept[:, layer] = jnp.where(first, one, other).reshape(SIDE // 8, 8, half)
        sent[:, layer] = jnp.where(first, other, one).reshape(SIDE // 8, 8, half)
    line = lax.broadcasted_iota(jnp.int32, (8, half), 0)
    last = lax.broadcasted_iota(jnp.int32, (8, half), 1) == half - 1
    spots = jnp.zeros((8, half), jnp.int32)
    for k in range(4):
        spots = jnp.where((line & 3) == k, own[k // 2, k % 2], spots)
    spots = spots.astype(jnp.float32)

    def step(part, inside):
        total = jnp.zeros((SIDE, SIDE), jnp.float32)
        for k in range(2):
            chi_real = chi[k * SIDE : (k + 1) * SIDE, :SIDE]
            chi_imag = chi[k * SIDE : (k + 1) * SIDE, SIDE:]
            pr, pi = rolled_probe[k, 0], rolled_probe[k, 1]
            term = pr * chi_imag - pi * chi_real if part else pr * chi_real + pi * chi_imag
            total += jnp.where(inside(*quadrants(own[k, 0], own[k, 1])), term, 0.0)
        return total

    for part in range(2):
        near_row[0, part] = step(part, lambda below, right: below & jnp.logical_not(right))
        near_row[1, part] = step(part, lambda below, right: below & right)
    near_row[1, 0, :8, half:] = jnp.where(last & (line < 4), spots, near_row[1, 0, :8, half:])
    store = pltpu.make_async_copy(near_row, step_row, stored)
    store.start()
    for part in range(2):
        step_right[part] = step(part, lambda below, right: right & jnp.logical_not(below))
        step_own[part] = step(part, lambda below, right: jnp.logical_not(below | right))
    step_right[0, :8, half:] = jnp.where(last & (line >= 4), spots, step_right[0, :8, half:])
    store.wait()


def vmem():
    return pl.BlockSpec(memory_space=pltpu.VMEM)


def smem():
    return pl.BlockSpec(memory_space=pltpu.SMEM)


def shape(*sizes):
    return jax.ShapeDtypeStruct(sizes, jnp.float32)


def anywhere():
    return pl.BlockSpec(memory_space=pl.ANY)


def prepare(own, probe):
    return pl.pallas_call(
        prepare_kernel,
        out_shape=shape(2, 2, SIDE, SIDE),
        in_specs=[smem(), vmem()],
        out_specs=vmem(),
        cost_estimate=pl.CostEstimate(flops=2000000, bytes_accessed=2 << 20, transcendentals=0),
        compiler_params=pltpu.CompilerParams(vmem_limit_bytes=16 << 20),
    )(own, probe)


def finish(own, probe, tile, step_own, step_row, step_right):
    return pl.pallas_call(
        finish_kernel,
        out_shape=shape(2, SIDE, SIDE),
        in_specs=[smem()] + [vmem()] * 5,
        out_specs=vmem(),
        cost_estimate=pl.CostEstimate(flops=8000000, bytes_accessed=8 << 20, transcendentals=0),
        compiler_params=pltpu.CompilerParams(vmem_limit_bytes=16 << 20),
    )(own, probe, tile, step_own, step_row, step_right)


def visit(own, core, tile, right_real, right_imag, below_tile, corner_real, corner_imag, rolled_probe, amplitude, tables):
    rows = SIDE // 8
    out_shape = (
        shape(rows, 3, 8, SIDE // 2),
        shape(rows, 3, 8, SIDE // 2),
        shape(2, SIDE, SIDE),
        shape(2, SIDE, SIDE),
        shape(2, 2, SIDE, SIDE),
    )
    return pl.pallas_call(
        visit_kernel,
        out_shape=out_shape,
        in_specs=[smem(), smem()] + [vmem()] * 9,
        out_specs=(vmem(),) * 4 + (anywhere(),),
        scratch_shapes=[pltpu.VMEM(rolled_probe.shape, jnp.float32)] * 2 + [pltpu.SemaphoreType.DMA],
        cost_estimate=pl.CostEstimate(flops=24 * 2 * 256**3 * 4, bytes_accessed=8 << 20, transcendentals=131072),
        compiler_params=pltpu.CompilerParams(vmem_limit_bytes=16 << 20),
    )(own, core, tile, right_real, right_imag, below_tile, corner_real, corner_imag, rolled_probe, amplitude, tables)


def fold_kernel(parts, copies):
    total = parts[...].sum(0)
    for k in range(copies.shape[0]):
        copies[k] = total


def fold(parts, count):
    return pl.pallas_call(
        fold_kernel,
        out_shape=shape(count, *parts.shape[1:]),
        in_specs=[vmem()],
        out_specs=vmem(),
        cost_estimate=pl.CostEstimate(flops=100000, bytes_accessed=1 << 19, transcendentals=0),
        compiler_params=pltpu.CompilerParams(vmem_limit_bytes=8 << 20),
    )(parts)


def settle_kernel(parts, corner, copies):
    total = parts[...].sum(0)
    new = [corner[part] + total[8 * part : 8 * part + 8] / (total[16:] + 1.0) for part in range(2)]
    both = jnp.concatenate(new, 0)
    for k in range(copies.shape[0]):
        copies[k] = both


def settle(parts, corner, count):
    return pl.pallas_call(
        settle_kernel,
        out_shape=shape(count, 16, SIDE // 2),
        in_specs=[vmem(), vmem()],
        out_specs=vmem(),
        cost_estimate=pl.CostEstimate(flops=100000, bytes_accessed=1 << 19, transcendentals=0),
        compiler_params=pltpu.CompilerParams(vmem_limit_bytes=8 << 20),
    )(parts, corner)


def body(positions, measured, object_field, probe):
    own = positions[0, 0]
    core = lax.axis_index("c")
    corner = lax.dynamic_slice(probe, (0, lax.axis_index(PLANE) * 8, core * (SIDE // 2)), (2, 8, SIDE // 2))
    right_real = passed_along(object_field[0], COL, -1)
    right_imag = passed_along(object_field[1], COL, -1)
    below_tile = passed_along(object_field, ROW, -1)
    rolled_probe = prepare(own, probe)
    right_real, rolled_probe, corner = lax.optimization_barrier((right_real, rolled_probe, corner))
    corner_real = passed_along(right_real, ROW, -1)
    corner_imag = passed_along(right_imag, ROW, -1)
    kept, sent, step_own, step_right, step_row = visit(
        own, core[None], object_field, right_real, right_imag, below_tile, corner_real, corner_imag, rolled_probe,
        measured[0, 0], jnp.asarray(dft_tables()),
    )
    other = lax.ppermute(sent, "c", [(0, 1), (1, 0)])
    rows = SIDE // 8
    pair = (kept + other).reshape(rows, 24, SIDE // 2)
    pair, step_row = lax.optimization_barrier((pair, step_row))
    summed = lax.all_to_all(pair, PLANE, 0, 0)
    step_row = passed_along(step_row, ROW, 1)
    summed = lax.all_to_all(fold(summed, lax.axis_size("y")), "y", 0, 0)
    step_right = passed_along(step_right + step_row[1], COL, 1)
    summed, step_row = lax.optimization_barrier((summed, step_row))
    near = lax.all_to_all(settle(summed, corner, rows), PLANE, 0, 0)
    new_object = finish(own, probe, object_field, step_own, step_row, step_right)
    near, new_object = lax.optimization_barrier((near, new_object))
    far = lax.ppermute(near, "c", [(0, 1), (1, 0)])
    pair = jnp.where(core == 0, jnp.stack([near, far]), jnp.stack([far, near]))
    new_probe = pair.reshape(2, rows, 2, 8, SIDE // 2).transpose(2, 1, 3, 0, 4).reshape(2, SIDE, SIDE)
    return (new_object, new_probe)


def solution(mesh):
    split = Mesh(mesh.devices.reshape(8, 2, 2, 2, 8), ROW + COL)
    in_specs = (P(ROW, COL), P(ROW, COL), P(None, ROW, COL), P())
    out_specs = (P(None, ROW, COL), P())
    return jax.shard_map(body, mesh=split, in_specs=in_specs, out_specs=out_specs, check_vma=False)
```

time: 132 us -> 112 us (0.85)
  starting transfers between devices: 76.9 us -> 47.3 us
  blocking collectives: 0 us -> 29.3 us
  waiting for transfers between devices: 31.1 us -> 19.1 us
  local copies, waits for them, and re-layouts: 9.19 us -> 1.84 us
  other arithmetic: 5.48 us -> 1.73 us
  Pallas kernels: 7.81 us -> 11.1 us
    all_to_all x0 -> x1, blocking collectives: none -> 29.3 us  [body(): summed = lax.all_to_all(pair, PLANE, 0, 0)]
    all_to_all x3 -> x2, starting transfers between devices: 35.1 us -> 12.4 us  [the longest x1 6.5 us: body(): near = lax.all_to_all(settle(summed, corner, rows), PLANE, 0, 0)]
    all_to_all x3 -> x2, waiting for transfers between devices: 28.6 us -> 7.77 us  [the longest x1 5.14 us: body(): near = lax.all_to_all(settle(summed, corner, rows), PLANE, 0, 0)]
    ppermute x8 -> x7, starting transfers between devices: 37.8 us -> 27.4 us  [passed_along(): lax.ppermute(value, axis, [(source, source + steps) for source in range(l...]
    unnamed x18 -> x10, local copies, waits for them, and re-layouts: 7.81 us -> 0.68 us
    ppermute x8 -> x7, waiting for transfers between devices: 2.41 us -> 8.51 us  [passed_along(): lax.ppermute(value, axis, [(source, source + steps) for source in range(l...]
    ppermute x1, starting transfers between devices: 1.91 us -> 5.58 us  [body(): far = lax.ppermute(near, 'c', [(0, 1), (1, 0)])]
    pallas_call x2 -> x5, Pallas kernels: 7.81 us -> 11.1 us  [the longest x1 6.33 us: visit(): pl.pallas_call(visit_kernel, out_shape=out_shape, in_specs=[smem(), smem(...]
  transfers between devices with their start and end apart: 13 -> 11, of which waited for: 5 -> 7; matrix products, arithmetic and copies ran while one was open for 5% -> 1% of each run, Pallas kernels for 1% -> 4%
where the time goes in v2:
time: 112 us; the launch traced here: 111 us
  starting transfers between devices  47.3 us (42%)
  blocking collectives  29.3 us (26%)
  waiting for transfers between devices  19.1 us (17%)
  Pallas kernels  11.1 us (10%)
  local copies, waits for them, and re-layouts  1.84 us (2%)
  other arithmetic  1.73 us (2%)
    all_to_all x1, blocking collectives, body(): summed = lax.all_to_all(pair, PLANE, 0, 0)  29.3 us
    ppermute x7, starting transfers between devices, passed_along(): lax.ppermute(value, axis, [(source, source + steps) for source in range(l...  27.4 us
    ppermute x7, waiting for transfers between devices, passed_along(): lax.ppermute(value, axis, [(source, source + steps) for source in range(l...  8.51 us
    all_to_all x1, starting transfers between devices, body(): near = lax.all_to_all(settle(summed, corner, rows), PLANE, 0, 0)  6.5 us
    pallas_call x1, Pallas kernels, visit(): pl.pallas_call(visit_kernel, out_shape=out_shape, in_specs=[smem(), smem(...  6.33 us
    all_to_all x1, starting transfers between devices, body(): summed = lax.all_to_all(fold(summed, lax.axis_size('y')), 'y', 0, 0)  5.92 us
    ppermute x1, starting transfers between devices, body(): far = lax.ppermute(near, 'c', [(0, 1), (1, 0)])  5.58 us
    all_to_all x1, waiting for transfers between devices, body(): near = lax.all_to_all(settle(summed, corner, rows), PLANE, 0, 0)  5.14 us
  transfers between devices with their start and end apart: 11, of which 7 were waited for; matrix products, arithmetic and copies ran while one was open for 1% of the time, Pallas kernels for 4%

profile of v2, /device:TPU:1, one launch (start us, length us, event | category | flops | bytes accessed | tf_op | source)
XLA Modules:
  0.0 111.2 jit_solution(14960353107478333357)
XLA Ops:
  0.6 1.2 %slice_bitcast_fusion.1 = (f32[256,256]{1,0:T(8,128)S(1)}, f32[256,256]{1,0:T(8,128)S(1)}) fusion(f32[2,256,256]{2,1,0:T(8,128)} %tile.3), kind=kLoop, calls=%fused_computation.6 | loop fusion | bytes 1048576 | tf_op jit(solution)/shard_map/squeeze | solution.py:283
  1.8 1.3 %collective-permute-start = (f32[256,256]{1,0:T(8,128)S(1)}, f32[256,256]{1,0:T(8,128)S(1)}, u32[]{:S(2)}, u32[]{:S(2)}) collective-permute-start(f32[256,256]{1,0:T(8,128)S(1)} %get-tuple-element.31), channel_id=1, source_target_pairs={{1,0},{2,1},{3,2},{4,3},{5,4},{6,5},{7,6},{8,7},{9,8},{10,9},{11,1... | collective-permute-start | bytes 786440 | tf_op jit(solution)/shard_map/ppermute | solution.py:22
  3.1 1.3 %collective-permute-start.1 = (f32[256,256]{1,0:T(8,128)S(1)}, f32[256,256]{1,0:T(8,128)S(1)}, u32[]{:S(2)}, u32[]{:S(2)}) collective-permute-start(f32[256,256]{1,0:T(8,128)S(1)} %get-tuple-element.30), channel_id=1, source_target_pairs={{1,0},{2,1},{3,2},{4,3},{5,4},{6,5},{7,6},{8,7},{9,8},{10,9},{11,1... | collective-permute-start | bytes 786440 | tf_op jit(solution)/shard_map/ppermute | solution.py:22
  4.4 8.8 %collective-permute-start.2 = (f32[2,256,256]{2,1,0:T(8,128)S(1)}, f32[2,256,256]{2,1,0:T(8,128)S(1)}, u32[]{:S(2)}, u32[]{:S(2)}) collective-permute-start(f32[2,256,256]{2,1,0:T(8,128)S(1)} %copy-done.1), channel_id=1, source_target_pairs={{16,0},{32,16},{48,32},{64,48},{80,64},{96,80},{112,96},{128,112},... | collective-permute-start | bytes 1572872 | tf_op jit(solution)/shard_map/ppermute | solution.py:22
  13.2 0.0 copy-start.2
  13.2 0.7 copy-done.2
  13.9 0.9 shard_map.68.rolled_probe
  14.9 0.0 collective-permute-done.right_real
  14.9 4.0 %collective-permute-start.3 = (f32[256,256]{1,0:T(8,128)S(1)}, f32[256,256]{1,0:T(8,128)S(1)}, u32[]{:S(2)}, u32[]{:S(2)}) collective-permute-start(f32[256,256]{1,0:T(8,128)S(1)} %collective-permute-done.right_real), channel_id=1, source_target_pairs={{16,0},{32,16},{48,32},{64,48},{80,64},{96,80},{112,96},{128,112},... | collective-permute-start | bytes 786440 | tf_op jit(solution)/shard_map/ppermute | solution.py:22
  18.9 0.0 collective-permute-done.1.right_imag
  18.9 2.8 %collective-permute-start.4 = (f32[256,256]{1,0:T(8,128)S(1)}, f32[256,256]{1,0:T(8,128)S(1)}, u32[]{:S(2)}, u32[]{:S(2)}) collective-permute-start(f32[256,256]{1,0:T(8,128)S(1)} %collective-permute-done.1.right_imag), channel_id=1, source_target_pairs={{16,0},{32,16},{48,32},{64,48},{80,64},{96,80},{112,96},{128,112},... | collective-permute-start | bytes 786440 | tf_op jit(solution)/shard_map/ppermute | solution.py:22
  21.7 2.4 %collective-permute-done.3.corner_real = f32[256,256]{1,0:T(8,128)S(1)} collective-permute-done((f32[256,256]{1,0:T(8,128)S(1)}, f32[256,256]{1,0:T(8,128)S(1)}, u32[]{:S(2)}, u32[]{:S(2)}) %collective-permute-start.3) | collective-permute-done | bytes 262176 | tf_op jit(solution)/shard_map/ppermute | solution.py:22
  24.1 4.0 %collective-permute-done.4.corner_imag = f32[256,256]{1,0:T(8,128)S(1)} collective-permute-done((f32[256,256]{1,0:T(8,128)S(1)}, f32[256,256]{1,0:T(8,128)S(1)}, u32[]{:S(2)}, u32[]{:S(2)}) %collective-permute-start.4) | collective-permute-done | bytes 262176 | tf_op jit(solution)/shard_map/ppermute | solution.py:22
  28.1 6.3 %shard_map.69 = (f32[32,3,8,128]{3,2,1,0:T(8,128)S(1)}, f32[32,3,8,128]{3,2,1,0:T(8,128)S(1)}, f32[2,256,256]{2,1,0:T(8,128)S(1)}, f32[2,256,256]{2,1,0:T(8,128)S(1)}, f32[2,2,256,256]{3,2,1,0:T(8,128)}) custom-call(s32[2,2]{1,0:T(2,128)S(1)} %bitcast.21, s32[1]{0:T(128)} %bitcast.1.core, f32[2,256,256]{2,1,0:T(8,128)S(1)} %copy-done.1, ...), custom_call_target="tpu_custom_call" | custom-call | flops 3221225472 | bytes 8388608 | tf_op jit(solution)/shard_map/pallas_call | solution.py:231
  34.4 1.9 %collective-permute-start.5 = (f32[32,3,8,128]{3,2,1,0:T(8,128)S(1)}, f32[32,3,8,128]{3,2,1,0:T(8,128)S(1)}, u32[]{:S(2)}, u32[]{:S(2)}) collective-permute-start(f32[32,3,8,128]{3,2,1,0:T(8,128)S(1)} %get-tuple-element.19), channel_id=1, source_target_pairs={{0,16},{16,0},{1,17},{17,1},{2,18},{18,2},{3,19},{19,3},{4,20},{20... | collective-permute-start | bytes 1179656 | tf_op jit(solution)/shard_map/ppermute | solution.py:293
  36.4 1.7 %collective-permute-done.5 = f32[32,3,8,128]{3,2,1,0:T(8,128)S(1)} collective-permute-done((f32[32,3,8,128]{3,2,1,0:T(8,128)S(1)}, f32[32,3,8,128]{3,2,1,0:T(8,128)S(1)}, u32[]{:S(2)}, u32[]{:S(2)}) %collective-permute-start.5) | collective-permute-done | bytes 393248 | tf_op jit(solution)/shard_map/ppermute | solution.py:293
  38.1 5.0 %collective-permute-start.6 = (f32[2,2,256,256]{3,2,1,0:T(8,128)}, f32[2,2,256,256]{3,2,1,0:T(8,128)S(1)}, u32[]{:S(2)}, u32[]{:S(2)}) collective-permute-start(f32[2,2,256,256]{3,2,1,0:T(8,128)} %get-tuple-element.22), channel_id=1, source_target_pairs={{0,16},{16,32},{32,48},{48,64},{64,80},{80,96},{96,112},{112,128},... | collective-permute-start | bytes 3145736 | tf_op jit(solution)/shard_map/ppermute | solution.py:22
  43.0 29.3 %all_to_all.15.parts = f32[32,24,128]{2,1,0:T(8,128)S(1)} all-to-all(f32[32,24,128]{2,1,0:T(8,128)S(1)} %add_bitcast_fusion), channel_id=1, replica_groups=mesh['y'=8,'xh'=2,'c'=2,'xl'=2,'z'=8] {'xh','xl','z'}, dimensions={0} | all-to-all | bytes 786432 | tf_op jit(solution)/shard_map/all_to_all | solution.py:297
  72.3 0.7 shard_map.70
  73.0 5.9 %all-to-all-start.1 = ((f32[8,24,128]{2,1,0:T(8,128)}), f32[8,24,128]{2,1,0:T(8,128)S(1)}, u32[]{:S(2)}, u32[]{:S(2)}) async-start(f32[8,24,128]{2,1,0:T(8,128)} %shard_map.70), calls=%async_computation.1 | async-start | bytes 196608 | tf_op jit(solution)/shard_map/all_to_all | solution.py:299
  79.0 0.0 collective-permute-done.6.step_row
  79.0 0.9 fusion
  79.8 4.3 %collective-permute-start.7 = (f32[2,256,256]{2,1,0:T(8,128)}, f32[2,256,256]{2,1,0:T(8,128)S(1)}, u32[]{:S(2)}, u32[]{:S(2)}) collective-permute-start(f32[2,256,256]{2,1,0:T(8,128)} %fusion), channel_id=1, source_target_pairs={{0,1},{1,2},{2,3},{3,4},{4,5},{5,6},{6,7},{7,8},{8,9},{9,10},{10,1... | collective-permute-start | bytes 1572872 | tf_op jit(solution)/shard_map/ppermute | solution.py:22
  84.1 2.6 %all-to-all-done.1.parts = f32[8,24,128]{2,1,0:T(8,128)S(1)} async-done(((f32[8,24,128]{2,1,0:T(8,128)}), f32[8,24,128]{2,1,0:T(8,128)S(1)}, u32[]{:S(2)}, u32[]{:S(2)}) %all-to-all-start.1) | async-done | bytes 98336 | tf_op jit(solution)/shard_map/all_to_all | solution.py:299
  86.7 0.7 shard_map.71
  87.5 6.5 %all-to-all-start.2 = ((f32[32,16,128]{2,1,0:T(8,128)}), f32[32,16,128]{2,1,0:T(8,128)S(1)}, u32[]{:S(2)}, u32[]{:S(2)}) async-start(f32[32,16,128]{2,1,0:T(8,128)} %shard_map.71), calls=%async_computation.2 | async-start | bytes 524288 | tf_op jit(solution)/shard_map/all_to_all | solution.py:302
  94.0 2.1 %collective-permute-done.7.step_right = f32[2,256,256]{2,1,0:T(8,128)S(1)} collective-permute-done((f32[2,256,256]{2,1,0:T(8,128)}, f32[2,256,256]{2,1,0:T(8,128)S(1)}, u32[]{:S(2)}, u32[]{:S(2)}) %collective-permute-start.7) | collective-permute-done | bytes 524320 | tf_op jit(solution)/shard_map/ppermute | solution.py:22
  96.1 2.4 %shard_map.72 = f32[2,256,256]{2,1,0:T(8,128)} custom-call(s32[2,2]{1,0:T(2,128)S(1)} %bitcast.22, f32[2,256,256]{2,1,0:T(8,128)S(1)} %copy-done, f32[2,256,256]{2,1,0:T(8,128)S(1)} %copy-done.1, f32[2,256,256]{2,1,0:T(8,128)S(1)} %get-tuple-element.25.step_own, f32[2,2,256,256]{3,2,1,0:T(8,128)S(1)} %collective-permute-done.6.step_row, ...), custom_call_target="tpu_custom_call" | custom-call | flops 8000000 | bytes 8388608 | tf_op jit(solution)/shard_map/pallas_call | solution.py:212
  98.5 5.1 %all-to-all-done.2 = f32[32,16,128]{2,1,0:T(8,128)S(1)} async-done(((f32[32,16,128]{2,1,0:T(8,128)}), f32[32,16,128]{2,1,0:T(8,128)S(1)}, u32[]{:S(2)}, u32[]{:S(2)}) %all-to-all-start.2) | async-done | bytes 262176 | tf_op jit(solution)/shard_map/all_to_all | solution.py:302
  103.6 5.6 %collective-permute-start.8 = (f32[32,16,128]{2,1,0:T(8,128)S(1)}, f32[32,16,128]{2,1,0:T(8,128)S(1)}, u32[]{:S(2)}, u32[]{:S(2)}) collective-permute-start(f32[32,16,128]{2,1,0:T(8,128)S(1)} %all-to-all-done.2), channel_id=1, source_target_pairs={{0,16},{16,0},{1,17},{17,1},{2,18},{18,2},{3,19},{19,3},{4,20},{20... | collective-permute-start | bytes 786440 | tf_op jit(solution)/shard_map/ppermute | solution.py:305
  109.2 1.1 %collective-permute-done.8 = f32[32,16,128]{2,1,0:T(8,128)S(1)} collective-permute-done((f32[32,16,128]{2,1,0:T(8,128)S(1)}, f32[32,16,128]{2,1,0:T(8,128)S(1)}, u32[]{:S(2)}, u32[]{:S(2)}) %collective-permute-start.8) | collective-permute-done | bytes 262176 | tf_op jit(solution)/shard_map/ppermute | solution.py:305
  110.4 0.8 copy_bitcast_fusion
  (11 shorter events, 0.1 us)
Async XLA Ops:
  0.6 3.8 %copy-start.1 = (f32[2,256,256]{2,1,0:T(8,128)S(1)}, f32[2,256,256]{2,1,0:T(8,128)}, u32[]{:S(2)}) copy-start(f32[2,256,256]{2,1,0:T(8,128)} %tile.3) | copy-start | bytes 1572868
  0.6 12.6 %copy-start = (f32[2,256,256]{2,1,0:T(8,128)S(1)}, f32[2,256,256]{2,1,0:T(8,128)}, u32[]{:S(2)}) copy-start(f32[2,256,256]{2,1,0:T(8,128)} %probe.3) | copy-start | bytes 1572868
  1.8 13.1 %collective-permute-start = (f32[256,256]{1,0:T(8,128)S(1)}, f32[256,256]{1,0:T(8,128)S(1)}, u32[]{:S(2)}, u32[]{:S(2)}) collective-permute-start(f32[256,256]{1,0:T(8,128)S(1)} %get-tuple-element.31), channel_id=1, source_target_pairs={{1,0},{2,1},{3,2},{4,3},{5,4},{6,5},{7,6},{8,7},{9,8},{10,9},{11,1... | collective-permute-start | bytes 786440 | tf_op jit(solution)/shard_map/ppermute | solution.py:22
  3.1 15.8 %collective-permute-start.1 = (f32[256,256]{1,0:T(8,128)S(1)}, f32[256,256]{1,0:T(8,128)S(1)}, u32[]{:S(2)}, u32[]{:S(2)}) collective-permute-start(f32[256,256]{1,0:T(8,128)S(1)} %get-tuple-element.30), channel_id=1, source_target_pairs={{1,0},{2,1},{3,2},{4,3},{5,4},{6,5},{7,6},{8,7},{9,8},{10,9},{11,1... | collective-permute-start | bytes 786440 | tf_op jit(solution)/shard_map/ppermute | solution.py:22
  4.4 23.7 %collective-permute-start.2 = (f32[2,256,256]{2,1,0:T(8,128)S(1)}, f32[2,256,256]{2,1,0:T(8,128)S(1)}, u32[]{:S(2)}, u32[]{:S(2)}) collective-permute-start(f32[2,256,256]{2,1,0:T(8,128)S(1)} %copy-done.1), channel_id=1, source_target_pairs={{16,0},{32,16},{48,32},{64,48},{80,64},{96,80},{112,96},{128,112},... | collective-permute-start | bytes 1572872 | tf_op jit(solution)/shard_map/ppermute | solution.py:22
  13.2 0.7 copy-start.2
  13.9 14.2 %copy-start.3 = (bf16[1,1,2,256,256]{4,3,2,1,0:T(8,128)(2,1)S(1)}, bf16[1,1,2,256,256]{4,3,2,1,0:T(8,128)(2,1)}, u32[]{:S(2)}) copy-start(bf16[1,1,2,256,256]{4,3,2,1,0:T(8,128)(2,1)} %param.6) | copy-start | bytes 786436
  13.9 14.2 %copy-start.4 = (bf16[3,2,256,256]{3,2,1,0:T(8,128)(2,1)S(1)}, bf16[3,2,256,256]{3,2,1,0:T(8,128)(2,1)}, u32[]{:S(2)}) copy-start(bf16[3,2,256,256]{3,2,1,0:T(8,128)(2,1)} %constant.29.clone.tables) | copy-start | bytes 2359300
  14.9 9.2 %collective-permute-start.3 = (f32[256,256]{1,0:T(8,128)S(1)}, f32[256,256]{1,0:T(8,128)S(1)}, u32[]{:S(2)}, u32[]{:S(2)}) collective-permute-start(f32[256,256]{1,0:T(8,128)S(1)} %collective-permute-done.right_real), channel_id=1, source_target_pairs={{16,0},{32,16},{48,32},{64,48},{80,64},{96,80},{112,96},{128,112},... | collective-permute-start | bytes 786440 | tf_op jit(solution)/shard_map/ppermute | solution.py:22
  18.9 9.2 %collective-permute-start.4 = (f32[256,256]{1,0:T(8,128)S(1)}, f32[256,256]{1,0:T(8,128)S(1)}, u32[]{:S(2)}, u32[]{:S(2)}) collective-permute-start(f32[256,256]{1,0:T(8,128)S(1)} %collective-permute-done.1.right_imag), channel_id=1, source_target_pairs={{16,0},{32,16},{48,32},{64,48},{80,64},{96,80},{112,96},{128,112},... | collective-permute-start | bytes 786440 | tf_op jit(solution)/shard_map/ppermute | solution.py:22
  34.4 3.6 %collective-permute-start.5 = (f32[32,3,8,128]{3,2,1,0:T(8,128)S(1)}, f32[32,3,8,128]{3,2,1,0:T(8,128)S(1)}, u32[]{:S(2)}, u32[]{:S(2)}) collective-permute-start(f32[32,3,8,128]{3,2,1,0:T(8,128)S(1)} %get-tuple-element.19), channel_id=1, source_target_pairs={{0,16},{16,0},{1,17},{17,1},{2,18},{18,2},{3,19},{19,3},{4,20},{20... | collective-permute-start | bytes 1179656 | tf_op jit(solution)/shard_map/ppermute | solution.py:293
  38.1 40.9 %collective-permute-start.6 = (f32[2,2,256,256]{3,2,1,0:T(8,128)}, f32[2,2,256,256]{3,2,1,0:T(8,128)S(1)}, u32[]{:S(2)}, u32[]{:S(2)}) collective-permute-start(f32[2,2,256,256]{3,2,1,0:T(8,128)} %get-tuple-element.22), channel_id=1, source_target_pairs={{0,16},{16,32},{32,48},{48,64},{64,80},{80,96},{96,112},{112,128},... | collective-permute-start | bytes 3145736 | tf_op jit(solution)/shard_map/ppermute | solution.py:22
  73.0 13.7 %all-to-all-start.1 = ((f32[8,24,128]{2,1,0:T(8,128)}), f32[8,24,128]{2,1,0:T(8,128)S(1)}, u32[]{:S(2)}, u32[]{:S(2)}) async-start(f32[8,24,128]{2,1,0:T(8,128)} %shard_map.70), calls=%async_computation.1 | async-start | bytes 196608 | tf_op jit(solution)/shard_map/all_to_all | solution.py:299
  79.8 16.2 %collective-permute-start.7 = (f32[2,256,256]{2,1,0:T(8,128)}, f32[2,256,256]{2,1,0:T(8,128)S(1)}, u32[]{:S(2)}, u32[]{:S(2)}) collective-permute-start(f32[2,256,256]{2,1,0:T(8,128)} %fusion), channel_id=1, source_target_pairs={{0,1},{1,2},{2,3},{3,4},{4,5},{5,6},{6,7},{7,8},{8,9},{9,10},{10,1... | collective-permute-start | bytes 1572872 | tf_op jit(solution)/shard_map/ppermute | solution.py:22
  87.5 16.2 %all-to-all-start.2 = ((f32[32,16,128]{2,1,0:T(8,128)}), f32[32,16,128]{2,1,0:T(8,128)S(1)}, u32[]{:S(2)}, u32[]{:S(2)}) async-start(f32[32,16,128]{2,1,0:T(8,128)} %shard_map.71), calls=%async_computation.2 | async-start | bytes 524288 | tf_op jit(solution)/shard_map/all_to_all | solution.py:302
  103.6 6.7 %collective-permute-start.8 = (f32[32,16,128]{2,1,0:T(8,128)S(1)}, f32[32,16,128]{2,1,0:T(8,128)S(1)}, u32[]{:S(2)}, u32[]{:S(2)}) collective-permute-start(f32[32,16,128]{2,1,0:T(8,128)S(1)} %all-to-all-done.2), channel_id=1, source_target_pairs={{0,16},{16,0},{1,17},{17,1},{2,18},{18,2},{3,19},{19,3},{4,20},{20... | collective-permute-start | bytes 786440 | tf_op jit(solution)/shard_map/ppermute | solution.py:305

commit v3 on v2

--- a/solution.py
+++ b/solution.py
@@ -251,7 +251,7 @@
         out_shape=shape(count, *parts.shape[1:]),
         in_specs=[vmem()],
         out_specs=vmem(),
-        cost_estimate=pl.CostEstimate(flops=100000, bytes_accessed=1 << 19, transcendentals=0),
+        cost_estimate=pl.CostEstimate(flops=4000000000, bytes_accessed=1 << 19, transcendentals=0),
         compiler_params=pltpu.CompilerParams(vmem_limit_bytes=8 << 20),
     )(parts)
 

time: 112 us -> 110 us (0.982)
  blocking collectives: 29.3 us -> 0 us
  starting transfers between devices: 47.3 us -> 67 us
  waiting for transfers between devices: 19.1 us -> 25.7 us
    all_to_all x1 -> x0, blocking collectives: 29.3 us -> none  [body(): summed = lax.all_to_all(pair, PLANE, 0, 0)]
    all_to_all x0 -> x1, starting transfers between devices: none -> 17 us  [body(): summed = lax.all_to_all(pair, PLANE, 0, 0)]
    all_to_all x0 -> x1, waiting for transfers between devices: none -> 6.91 us  [body(): summed = lax.all_to_all(pair, PLANE, 0, 0)]
    ppermute x7, waiting for transfers between devices: 8.51 us -> 6.43 us  [passed_along(): lax.ppermute(value, axis, [(source, source + steps) for source in range(l...]
    all_to_all x1, waiting for transfers between devices: 5.14 us -> 7.17 us  [body(): near = lax.all_to_all(settle(summed, corner, rows), PLANE, 0, 0)]
    all_to_all x1, starting transfers between devices: 5.92 us -> 7.27 us  [body(): summed = lax.all_to_all(fold(summed, lax.axis_size('y')), 'y', 0, 0)]
  transfers between devices with their start and end apart: 11 -> 12, of which waited for: 7 -> 7; matrix products, arithmetic and copies ran while one was open for 1% -> 1% of each run, Pallas kernels for 4% -> 4%
where the time goes in v3:
time: 110 us; the launch traced here: 109 us
  starting transfers between devices  67 us (61%)
  waiting for transfers between devices  25.7 us (23%)
  Pallas kernels  10.8 us (10%)
  local copies, waits for them, and re-layouts  2.48 us (2%)
  other arithmetic  2.48 us (2%)
    ppermute x7, starting transfers between devices, passed_along(): lax.ppermute(value, axis, [(source, source + steps) for source in range(l...  27.7 us
    all_to_all x1, starting transfers between devices, body(): summed = lax.all_to_all(pair, PLANE, 0, 0)  17 us
    all_to_all x1, starting transfers between devices, body(): summed = lax.all_to_all(fold(summed, lax.axis_size('y')), 'y', 0, 0)  7.27 us
    all_to_all x1, waiting for transfers between devices, body(): near = lax.all_to_all(settle(summed, corner, rows), PLANE, 0, 0)  7.17 us
    all_to_all x1, starting transfers between devices, body(): near = lax.all_to_all(settle(summed, corner, rows), PLANE, 0, 0)  7 us
    all_to_all x1, waiting for transfers between devices, body(): summed = lax.all_to_all(pair, PLANE, 0, 0)  6.91 us
    pallas_call x1, Pallas kernels, visit(): pl.pallas_call(visit_kernel, out_shape=out_shape, in_specs=[smem(), smem(...  6.61 us
    ppermute x7, waiting for transfers between devices, passed_along(): lax.ppermute(value, axis, [(source, source + steps) for source in range(l...  6.43 us
  transfers between devices with their start and end apart: 12, of which 7 were waited for; matrix products, arithmetic and copies ran while one was open for 1% of the time, Pallas kernels for 4%

profile of v3, /device:TPU:1, one launch (start us, length us, event | category | flops | bytes accessed | tf_op | source)
XLA Modules:
  0.0 109.3 jit_solution(5616489725249892345)
XLA Ops:
  0.6 1.2 %slice_bitcast_fusion.1 = (f32[256,256]{1,0:T(8,128)S(1)}, f32[256,256]{1,0:T(8,128)S(1)}) fusion(f32[2,256,256]{2,1,0:T(8,128)} %tile.3), kind=kLoop, calls=%fused_computation.6 | loop fusion | bytes 1048576 | tf_op jit(solution)/shard_map/squeeze | solution.py:283
  1.8 1.3 %collective-permute-start = (f32[256,256]{1,0:T(8,128)S(1)}, f32[256,256]{1,0:T(8,128)S(1)}, u32[]{:S(2)}, u32[]{:S(2)}) collective-permute-start(f32[256,256]{1,0:T(8,128)S(1)} %get-tuple-element.31), channel_id=1, source_target_pairs={{1,0},{2,1},{3,2},{4,3},{5,4},{6,5},{7,6},{8,7},{9,8},{10,9},{11,1... | collective-permute-start | bytes 786440 | tf_op jit(solution)/shard_map/ppermute | solution.py:22
  3.1 1.3 %collective-permute-start.1 = (f32[256,256]{1,0:T(8,128)S(1)}, f32[256,256]{1,0:T(8,128)S(1)}, u32[]{:S(2)}, u32[]{:S(2)}) collective-permute-start(f32[256,256]{1,0:T(8,128)S(1)} %get-tuple-element.30), channel_id=1, source_target_pairs={{1,0},{2,1},{3,2},{4,3},{5,4},{6,5},{7,6},{8,7},{9,8},{10,9},{11,1... | collective-permute-start | bytes 786440 | tf_op jit(solution)/shard_map/ppermute | solution.py:22
  4.4 8.8 %collective-permute-start.2 = (f32[2,256,256]{2,1,0:T(8,128)S(1)}, f32[2,256,256]{2,1,0:T(8,128)S(1)}, u32[]{:S(2)}, u32[]{:S(2)}) collective-permute-start(f32[2,256,256]{2,1,0:T(8,128)S(1)} %copy-done.1), channel_id=1, source_target_pairs={{16,0},{32,16},{48,32},{64,48},{80,64},{96,80},{112,96},{128,112},... | collective-permute-start | bytes 1572872 | tf_op jit(solution)/shard_map/ppermute | solution.py:22
  13.2 0.0 copy-start.3
  13.2 0.7 copy-done.3
  13.9 0.9 shard_map.68.rolled_probe
  14.9 0.0 collective-permute-done.right_real
  14.9 4.0 %collective-permute-start.3 = (f32[256,256]{1,0:T(8,128)S(1)}, f32[256,256]{1,0:T(8,128)S(1)}, u32[]{:S(2)}, u32[]{:S(2)}) collective-permute-start(f32[256,256]{1,0:T(8,128)S(1)} %collective-permute-done.right_real), channel_id=1, source_target_pairs={{16,0},{32,16},{48,32},{64,48},{80,64},{96,80},{112,96},{128,112},... | collective-permute-start | bytes 786440 | tf_op jit(solution)/shard_map/ppermute | solution.py:22
  18.9 2.8 %collective-permute-start.4 = (f32[256,256]{1,0:T(8,128)S(1)}, f32[256,256]{1,0:T(8,128)S(1)}, u32[]{:S(2)}, u32[]{:S(2)}) collective-permute-start(f32[256,256]{1,0:T(8,128)S(1)} %collective-permute-done.1.right_imag), channel_id=1, source_target_pairs={{16,0},{32,16},{48,32},{64,48},{80,64},{96,80},{112,96},{128,112},... | collective-permute-start | bytes 786440 | tf_op jit(solution)/shard_map/ppermute | solution.py:22
  21.7 2.4 %collective-permute-done.3.corner_real = f32[256,256]{1,0:T(8,128)S(1)} collective-permute-done((f32[256,256]{1,0:T(8,128)S(1)}, f32[256,256]{1,0:T(8,128)S(1)}, u32[]{:S(2)}, u32[]{:S(2)}) %collective-permute-start.3) | collective-permute-done | bytes 262176 | tf_op jit(solution)/shard_map/ppermute | solution.py:22
  24.1 4.0 %collective-permute-done.4.corner_imag = f32[256,256]{1,0:T(8,128)S(1)} collective-permute-done((f32[256,256]{1,0:T(8,128)S(1)}, f32[256,256]{1,0:T(8,128)S(1)}, u32[]{:S(2)}, u32[]{:S(2)}) %collective-permute-start.4) | collective-permute-done | bytes 262176 | tf_op jit(solution)/shard_map/ppermute | solution.py:22
  28.1 6.6 %shard_map.69 = (f32[32,3,8,128]{3,2,1,0:T(8,128)S(1)}, f32[32,3,8,128]{3,2,1,0:T(8,128)S(1)}, f32[2,256,256]{2,1,0:T(8,128)S(1)}, f32[2,256,256]{2,1,0:T(8,128)S(1)}, f32[2,2,256,256]{3,2,1,0:T(8,128)S(1)}) custom-call(s32[2,2]{1,0:T(2,128)S(1)} %bitcast.21, s32[1]{0:T(128)} %bitcast.1.core, f32[2,256,256]{2,1,0:T(8,128)S(1)} %copy-done.1, ...), custom_call_target="tpu_custom_call" | custom-call | flops 3221225472 | bytes 8388608 | tf_op jit(solution)/shard_map/pallas_call | solution.py:231
  34.7 1.9 %collective-permute-start.5 = (f32[32,3,8,128]{3,2,1,0:T(8,128)S(1)}, f32[32,3,8,128]{3,2,1,0:T(8,128)S(1)}, u32[]{:S(2)}, u32[]{:S(2)}) collective-permute-start(f32[32,3,8,128]{3,2,1,0:T(8,128)S(1)} %get-tuple-element.19), channel_id=1, source_target_pairs={{0,16},{16,0},{1,17},{17,1},{2,18},{18,2},{3,19},{19,3},{4,20},{20... | collective-permute-start | bytes 1179656 | tf_op jit(solution)/shard_map/ppermute | solution.py:293
  36.6 1.7 %collective-permute-done.5 = f32[32,3,8,128]{3,2,1,0:T(8,128)S(1)} collective-permute-done((f32[32,3,8,128]{3,2,1,0:T(8,128)S(1)}, f32[32,3,8,128]{3,2,1,0:T(8,128)S(1)}, u32[]{:S(2)}, u32[]{:S(2)}) %collective-permute-start.5) | collective-permute-done | bytes 393248 | tf_op jit(solution)/shard_map/ppermute | solution.py:293
  38.3 0.8 add_bitcast_fusion
  39.1 17.0 %all-to-all-start = ((f32[32,24,128]{2,1,0:T(8,128)}), f32[32,24,128]{2,1,0:T(8,128)S(1)}, u32[]{:S(2)}, u32[]{:S(2)}) async-start(f32[32,24,128]{2,1,0:T(8,128)} %add_bitcast_fusion), calls=%async_computation | async-start | bytes 786432 | tf_op jit(solution)/shard_map/all_to_all | solution.py:297
  56.1 5.2 %collective-permute-start.6 = (f32[2,2,256,256]{3,2,1,0:T(8,128)}, f32[2,2,256,256]{3,2,1,0:T(8,128)S(1)}, u32[]{:S(2)}, u32[]{:S(2)}) collective-permute-start(f32[2,2,256,256]{3,2,1,0:T(8,128)} %copy-done.4), channel_id=1, source_target_pairs={{0,16},{16,32},{32,48},{48,64},{64,80},{80,96},{96,112},{112,128},... | collective-permute-start | bytes 3145736 | tf_op jit(solution)/shard_map/ppermute | solution.py:22
  61.4 6.9 %all-to-all-done.parts = f32[32,24,128]{2,1,0:T(8,128)S(1)} async-done(((f32[32,24,128]{2,1,0:T(8,128)}), f32[32,24,128]{2,1,0:T(8,128)S(1)}, u32[]{:S(2)}, u32[]{:S(2)}) %all-to-all-start) | async-done | bytes 393248 | tf_op jit(solution)/shard_map/all_to_all | solution.py:297
  68.3 0.0 copy-start.2
  68.3 0.6 copy-done.2
  68.9 7.3 %all-to-all-start.1 = ((f32[8,24,128]{2,1,0:T(8,128)}), f32[8,24,128]{2,1,0:T(8,128)S(1)}, u32[]{:S(2)}, u32[]{:S(2)}) async-start(f32[8,24,128]{2,1,0:T(8,128)} %copy-done.2), calls=%async_computation.1 | async-start | bytes 196608 | tf_op jit(solution)/shard_map/all_to_all | solution.py:299
  76.2 0.9 fusion
  77.1 4.3 %collective-permute-start.7 = (f32[2,256,256]{2,1,0:T(8,128)}, f32[2,256,256]{2,1,0:T(8,128)S(1)}, u32[]{:S(2)}, u32[]{:S(2)}) collective-permute-start(f32[2,256,256]{2,1,0:T(8,128)} %fusion), channel_id=1, source_target_pairs={{0,1},{1,2},{2,3},{3,4},{4,5},{5,6},{6,7},{7,8},{8,9},{9,10},{10,1... | collective-permute-start | bytes 1572872 | tf_op jit(solution)/shard_map/ppermute | solution.py:22
  81.4 2.4 %all-to-all-done.1.parts = f32[8,24,128]{2,1,0:T(8,128)S(1)} async-done(((f32[8,24,128]{2,1,0:T(8,128)}), f32[8,24,128]{2,1,0:T(8,128)S(1)}, u32[]{:S(2)}, u32[]{:S(2)}) %all-to-all-start.1) | async-done | bytes 98336 | tf_op jit(solution)/shard_map/all_to_all | solution.py:299
  83.8 0.7 shard_map.71
  84.5 7.0 %all-to-all-start.2 = ((f32[32,16,128]{2,1,0:T(8,128)}), f32[32,16,128]{2,1,0:T(8,128)S(1)}, u32[]{:S(2)}, u32[]{:S(2)}) async-start(f32[32,16,128]{2,1,0:T(8,128)} %shard_map.71), calls=%async_computation.2 | async-start | bytes 524288 | tf_op jit(solution)/shard_map/all_to_all | solution.py:302
  91.6 2.5 %shard_map.72 = f32[2,256,256]{2,1,0:T(8,128)} custom-call(s32[2,2]{1,0:T(2,128)S(1)} %bitcast.22, f32[2,256,256]{2,1,0:T(8,128)S(1)} %copy-done, f32[2,256,256]{2,1,0:T(8,128)S(1)} %copy-done.1, f32[2,256,256]{2,1,0:T(8,128)S(1)} %get-tuple-element.25.step_own, f32[2,2,256,256]{3,2,1,0:T(8,128)S(1)} %collective-permute-done.6.step_row, ...), custom_call_target="tpu_custom_call" | custom-call | flops 8000000 | bytes 8388608 | tf_op jit(solution)/shard_map/pallas_call | solution.py:212
  94.0 7.2 %all-to-all-done.2 = f32[32,16,128]{2,1,0:T(8,128)S(1)} async-done(((f32[32,16,128]{2,1,0:T(8,128)}), f32[32,16,128]{2,1,0:T(8,128)S(1)}, u32[]{:S(2)}, u32[]{:S(2)}) %all-to-all-start.2) | async-done | bytes 262176 | tf_op jit(solution)/shard_map/all_to_all | solution.py:302
  101.2 6.1 %collective-permute-start.8 = (f32[32,16,128]{2,1,0:T(8,128)S(1)}, f32[32,16,128]{2,1,0:T(8,128)S(1)}, u32[]{:S(2)}, u32[]{:S(2)}) collective-permute-start(f32[32,16,128]{2,1,0:T(8,128)S(1)} %all-to-all-done.2), channel_id=1, source_target_pairs={{0,16},{16,0},{1,17},{17,1},{2,18},{18,2},{3,19},{19,3},{4,20},{20... | collective-permute-start | bytes 786440 | tf_op jit(solution)/shard_map/ppermute | solution.py:305
  107.3 1.1 %collective-permute-done.8 = f32[32,16,128]{2,1,0:T(8,128)S(1)} collective-permute-done((f32[32,16,128]{2,1,0:T(8,128)S(1)}, f32[32,16,128]{2,1,0:T(8,128)S(1)}, u32[]{:S(2)}, u32[]{:S(2)}) %collective-permute-start.8) | collective-permute-done | bytes 262176 | tf_op jit(solution)/shard_map/ppermute | solution.py:305
  108.5 0.8 copy_bitcast_fusion
  (16 shorter events, 0.1 us)
Async XLA Ops:
  0.6 3.8 %copy-start.1 = (f32[2,256,256]{2,1,0:T(8,128)S(1)}, f32[2,256,256]{2,1,0:T(8,128)}, u32[]{:S(2)}) copy-start(f32[2,256,256]{2,1,0:T(8,128)} %tile.3) | copy-start | bytes 1572868
  0.6 12.6 %copy-start = (f32[2,256,256]{2,1,0:T(8,128)S(1)}, f32[2,256,256]{2,1,0:T(8,128)}, u32[]{:S(2)}) copy-start(f32[2,256,256]{2,1,0:T(8,128)} %probe.3) | copy-start | bytes 1572868
  1.8 13.1 %collective-permute-start = (f32[256,256]{1,0:T(8,128)S(1)}, f32[256,256]{1,0:T(8,128)S(1)}, u32[]{:S(2)}, u32[]{:S(2)}) collective-permute-start(f32[256,256]{1,0:T(8,128)S(1)} %get-tuple-element.31), channel_id=1, source_target_pairs={{1,0},{2,1},{3,2},{4,3},{5,4},{6,5},{7,6},{8,7},{9,8},{10,9},{11,1... | collective-permute-start | bytes 786440 | tf_op jit(solution)/shard_map/ppermute | solution.py:22
  3.1 15.8 %collective-permute-start.1 = (f32[256,256]{1,0:T(8,128)S(1)}, f32[256,256]{1,0:T(8,128)S(1)}, u32[]{:S(2)}, u32[]{:S(2)}) collective-permute-start(f32[256,256]{1,0:T(8,128)S(1)} %get-tuple-element.30), channel_id=1, source_target_pairs={{1,0},{2,1},{3,2},{4,3},{5,4},{6,5},{7,6},{8,7},{9,8},{10,9},{11,1... | collective-permute-start | bytes 786440 | tf_op jit(solution)/shard_map/ppermute | solution.py:22
  4.4 23.7 %collective-permute-start.2 = (f32[2,256,256]{2,1,0:T(8,128)S(1)}, f32[2,256,256]{2,1,0:T(8,128)S(1)}, u32[]{:S(2)}, u32[]{:S(2)}) collective-permute-start(f32[2,256,256]{2,1,0:T(8,128)S(1)} %copy-done.1), channel_id=1, source_target_pairs={{16,0},{32,16},{48,32},{64,48},{80,64},{96,80},{112,96},{128,112},... | collective-permute-start | bytes 1572872 | tf_op jit(solution)/shard_map/ppermute | solution.py:22
  13.2 0.7 copy-start.3
  13.9 14.2 %copy-start.5 = (bf16[1,1,2,256,256]{4,3,2,1,0:T(8,128)(2,1)S(1)}, bf16[1,1,2,256,256]{4,3,2,1,0:T(8,128)(2,1)}, u32[]{:S(2)}) copy-start(bf16[1,1,2,256,256]{4,3,2,1,0:T(8,128)(2,1)} %param.6) | copy-start | bytes 786436
  13.9 14.2 %copy-start.6 = (bf16[3,2,256,256]{3,2,1,0:T(8,128)(2,1)S(1)}, bf16[3,2,256,256]{3,2,1,0:T(8,128)(2,1)}, u32[]{:S(2)}) copy-start(bf16[3,2,256,256]{3,2,1,0:T(8,128)(2,1)} %constant.29.clone.tables) | copy-start | bytes 2359300
  14.9 9.2 %collective-permute-start.3 = (f32[256,256]{1,0:T(8,128)S(1)}, f32[256,256]{1,0:T(8,128)S(1)}, u32[]{:S(2)}, u32[]{:S(2)}) collective-permute-start(f32[256,256]{1,0:T(8,128)S(1)} %collective-permute-done.right_real), channel_id=1, source_target_pairs={{16,0},{32,16},{48,32},{64,48},{80,64},{96,80},{112,96},{128,112},... | collective-permute-start | bytes 786440 | tf_op jit(solution)/shard_map/ppermute | solution.py:22
  18.9 9.2 %collective-permute-start.4 = (f32[256,256]{1,0:T(8,128)S(1)}, f32[256,256]{1,0:T(8,128)S(1)}, u32[]{:S(2)}, u32[]{:S(2)}) collective-permute-start(f32[256,256]{1,0:T(8,128)S(1)} %collective-permute-done.1.right_imag), channel_id=1, source_target_pairs={{16,0},{32,16},{48,32},{64,48},{80,64},{96,80},{112,96},{128,112},... | collective-permute-start | bytes 786440 | tf_op jit(solution)/shard_map/ppermute | solution.py:22
  34.7 4.4 %copy-start.4 = (f32[2,2,256,256]{3,2,1,0:T(8,128)}, f32[2,2,256,256]{3,2,1,0:T(8,128)S(1)}, u32[]{:S(2)}) copy-start(f32[2,2,256,256]{3,2,1,0:T(8,128)S(1)} %get-tuple-element.22) | copy-start | bytes 3145732
  34.7 3.6 %collective-permute-start.5 = (f32[32,3,8,128]{3,2,1,0:T(8,128)S(1)}, f32[32,3,8,128]{3,2,1,0:T(8,128)S(1)}, u32[]{:S(2)}, u32[]{:S(2)}) collective-permute-start(f32[32,3,8,128]{3,2,1,0:T(8,128)S(1)} %get-tuple-element.19), channel_id=1, source_target_pairs={{0,16},{16,0},{1,17},{17,1},{2,18},{18,2},{3,19},{19,3},{4,20},{20... | collective-permute-start | bytes 1179656 | tf_op jit(solution)/shard_map/ppermute | solution.py:293
  39.1 29.1 %all-to-all-start = ((f32[32,24,128]{2,1,0:T(8,128)}), f32[32,24,128]{2,1,0:T(8,128)S(1)}, u32[]{:S(2)}, u32[]{:S(2)}) async-start(f32[32,24,128]{2,1,0:T(8,128)} %add_bitcast_fusion), calls=%async_computation | async-start | bytes 786432 | tf_op jit(solution)/shard_map/all_to_all | solution.py:297
  56.1 20.1 %collective-permute-start.6 = (f32[2,2,256,256]{3,2,1,0:T(8,128)}, f32[2,2,256,256]{3,2,1,0:T(8,128)S(1)}, u32[]{:S(2)}, u32[]{:S(2)}) collective-permute-start(f32[2,2,256,256]{3,2,1,0:T(8,128)} %copy-done.4), channel_id=1, source_target_pairs={{0,16},{16,32},{32,48},{48,64},{64,80},{80,96},{96,112},{112,128},... | collective-permute-start | bytes 3145736 | tf_op jit(solution)/shard_map/ppermute | solution.py:22
  68.3 0.6 copy-start.2
  68.9 14.8 %all-to-all-start.1 = ((f32[8,24,128]{2,1,0:T(8,128)}), f32[8,24,128]{2,1,0:T(8,128)S(1)}, u32[]{:S(2)}, u32[]{:S(2)}) async-start(f32[8,24,128]{2,1,0:T(8,128)} %copy-done.2), calls=%async_computation.1 | async-start | bytes 196608 | tf_op jit(solution)/shard_map/all_to_all | solution.py:299
  77.1 14.5 %collective-permute-start.7 = (f32[2,256,256]{2,1,0:T(8,128)}, f32[2,256,256]{2,1,0:T(8,128)S(1)}, u32[]{:S(2)}, u32[]{:S(2)}) collective-permute-start(f32[2,256,256]{2,1,0:T(8,128)} %fusion), channel_id=1, source_target_pairs={{0,1},{1,2},{2,3},{3,4},{4,5},{5,6},{6,7},{7,8},{8,9},{9,10},{10,1... | collective-permute-start | bytes 1572872 | tf_op jit(solution)/shard_map/ppermute | solution.py:22
  84.5 16.7 %all-to-all-start.2 = ((f32[32,16,128]{2,1,0:T(8,128)}), f32[32,16,128]{2,1,0:T(8,128)S(1)}, u32[]{:S(2)}, u32[]{:S(2)}) async-start(f32[32,16,128]{2,1,0:T(8,128)} %shard_map.71), calls=%async_computation.2 | async-start | bytes 524288 | tf_op jit(solution)/shard_map/all_to_all | solution.py:302
  101.2 7.3 %collective-permute-start.8 = (f32[32,16,128]{2,1,0:T(8,128)S(1)}, f32[32,16,128]{2,1,0:T(8,128)S(1)}, u32[]{:S(2)}, u32[]{:S(2)}) collective-permute-start(f32[32,16,128]{2,1,0:T(8,128)S(1)} %all-to-all-done.2), channel_id=1, source_target_pairs={{0,16},{16,0},{1,17},{17,1},{2,18},{18,2},{3,19},{19,3},{4,20},{20... | collective-permute-start | bytes 786440 | tf_op jit(solution)/shard_map/ppermute | solution.py:305

commit v4 on v3

--- a/solution.py
+++ b/solution.py
@@ -111,7 +111,7 @@
 
 def visit_kernel(
     own, core, tile, right_real, right_imag, below_tile, corner_real, corner_imag, rolled_probe, amplitude,
-    tables, kept, sent, step_own, step_right, step_row, patches, near_row, stored,
+    tables, kept, sent, step_own, step_right, step_row, patches,
 ):
     right_tile, corner_tile = (right_real, right_imag), (corner_real, corner_imag)
     exits = []
@@ -169,16 +169,13 @@
         return total
 
     for part in range(2):
-        near_row[0, part] = step(part, lambda below, right: below & jnp.logical_not(right))
-        near_row[1, part] = step(part, lambda below, right: below & right)
-    near_row[1, 0, :8, half:] = jnp.where(last & (line < 4), spots, near_row[1, 0, :8, half:])
-    store = pltpu.make_async_copy(near_row, step_row, stored)
-    store.start()
+        step_row[0, part] = step(part, lambda below, right: below & jnp.logical_not(right))
+        step_row[1, part] = step(part, lambda below, right: below & right)
+    step_row[1, 0, :8, half:] = jnp.where(last & (line < 4), spots, step_row[1, 0, :8, half:])
     for part in range(2):
         step_right[part] = step(part, lambda below, right: right & jnp.logical_not(below))
         step_own[part] = step(part, lambda below, right: jnp.logical_not(below | right))
     step_right[0, :8, half:] = jnp.where(last & (line >= 4), spots, step_right[0, :8, half:])
-    store.wait()
 
 
 def vmem():
@@ -232,8 +229,8 @@
         visit_kernel,
         out_shape=out_shape,
         in_specs=[smem(), smem()] + [vmem()] * 9,
-        out_specs=(vmem(),) * 4 + (anywhere(),),
-        scratch_shapes=[pltpu.VMEM(rolled_probe.shape, jnp.float32)] * 2 + [pltpu.SemaphoreType.DMA],
+        out_specs=(vmem(),) * 5,
+        scratch_shapes=[pltpu.VMEM(rolled_probe.shape, jnp.float32)],
         cost_estimate=pl.CostEstimate(flops=24 * 2 * 256**3 * 4, bytes_accessed=8 << 20, transcendentals=131072),
         compiler_params=pltpu.CompilerParams(vmem_limit_bytes=16 << 20),
     )(own, core, tile, right_real, right_imag, below_tile, corner_real, corner_imag, rolled_probe, amplitude, tables)

time: 110 us -> 109 us (level)
  no operation moved by 1% of the time
where the time goes in v4:
time: 109 us
  starting transfers between devices  67 us (61%)
  waiting for transfers between devices  25.7 us (24%)
  Pallas kernels  10.1 us (9%)
  local copies, waits for them, and re-layouts  2.48 us (2%)
  other arithmetic  2.48 us (2%)
    ppermute x7, starting transfers between devices, passed_along(): lax.ppermute(value, axis, [(source, source + steps) for source in range(l...  27.7 us
    all_to_all x1, starting transfers between devices, body(): summed = lax.all_to_all(pair, PLANE, 0, 0)  17 us
    all_to_all x1, starting transfers between devices, body(): summed = lax.all_to_all(fold(summed, lax.axis_size('y')), 'y', 0, 0)  7.27 us
    all_to_all x1, waiting for transfers between devices, body(): near = lax.all_to_all(settle(summed, corner, rows), PLANE, 0, 0)  7.17 us
    all_to_all x1, starting transfers between devices, body(): near = lax.all_to_all(settle(summed, corner, rows), PLANE, 0, 0)  7 us
    all_to_all x1, waiting for transfers between devices, body(): summed = lax.all_to_all(pair, PLANE, 0, 0)  6.91 us
    ppermute x7, waiting for transfers between devices, passed_along(): lax.ppermute(value, axis, [(source, source + steps) for source in range(l...  6.43 us
    ppermute x1, starting transfers between devices, body(): far = lax.ppermute(near, 'c', [(0, 1), (1, 0)])  6.13 us
  transfers between devices with their start and end apart: 12, of which 7 were waited for; matrix products, arithmetic and copies ran while one was open for 1% of the time, Pallas kernels for 4%

profile of v4, /device:TPU:1, one launch (start us, length us, event | category | flops | bytes accessed | tf_op | source)
XLA Modules:
  0.0 108.6 jit_solution(18278950304280063989)
XLA Ops:
  0.6 1.2 %slice_bitcast_fusion.1 = (f32[256,256]{1,0:T(8,128)S(1)}, f32[256,256]{1,0:T(8,128)S(1)}) fusion(f32[2,256,256]{2,1,0:T(8,128)} %tile.3), kind=kLoop, calls=%fused_computation.6 | loop fusion | bytes 1048576 | tf_op jit(solution)/shard_map/squeeze | solution.py:280
  1.8 1.3 %collective-permute-start = (f32[256,256]{1,0:T(8,128)S(1)}, f32[256,256]{1,0:T(8,128)S(1)}, u32[]{:S(2)}, u32[]{:S(2)}) collective-permute-start(f32[256,256]{1,0:T(8,128)S(1)} %get-tuple-element.31), channel_id=1, source_target_pairs={{1,0},{2,1},{3,2},{4,3},{5,4},{6,5},{7,6},{8,7},{9,8},{10,9},{11,1... | collective-permute-start | bytes 786440 | tf_op jit(solution)/shard_map/ppermute | solution.py:22
  3.1 1.3 %collective-permute-start.1 = (f32[256,256]{1,0:T(8,128)S(1)}, f32[256,256]{1,0:T(8,128)S(1)}, u32[]{:S(2)}, u32[]{:S(2)}) collective-permute-start(f32[256,256]{1,0:T(8,128)S(1)} %get-tuple-element.30), channel_id=1, source_target_pairs={{1,0},{2,1},{3,2},{4,3},{5,4},{6,5},{7,6},{8,7},{9,8},{10,9},{11,1... | collective-permute-start | bytes 786440 | tf_op jit(solution)/shard_map/ppermute | solution.py:22
  4.4 8.8 %collective-permute-start.2 = (f32[2,256,256]{2,1,0:T(8,128)S(1)}, f32[2,256,256]{2,1,0:T(8,128)S(1)}, u32[]{:S(2)}, u32[]{:S(2)}) collective-permute-start(f32[2,256,256]{2,1,0:T(8,128)S(1)} %copy-done.1), channel_id=1, source_target_pairs={{16,0},{32,16},{48,32},{64,48},{80,64},{96,80},{112,96},{128,112},... | collective-permute-start | bytes 1572872 | tf_op jit(solution)/shard_map/ppermute | solution.py:22
  13.2 0.0 copy-start.3
  13.2 0.7 copy-done.3
  13.9 0.9 shard_map.68.rolled_probe
  14.9 0.0 collective-permute-done.right_real
  14.9 4.0 %collective-permute-start.3 = (f32[256,256]{1,0:T(8,128)S(1)}, f32[256,256]{1,0:T(8,128)S(1)}, u32[]{:S(2)}, u32[]{:S(2)}) collective-permute-start(f32[256,256]{1,0:T(8,128)S(1)} %collective-permute-done.right_real), channel_id=1, source_target_pairs={{16,0},{32,16},{48,32},{64,48},{80,64},{96,80},{112,96},{128,112},... | collective-permute-start | bytes 786440 | tf_op jit(solution)/shard_map/ppermute | solution.py:22
  18.9 2.8 %collective-permute-start.4 = (f32[256,256]{1,0:T(8,128)S(1)}, f32[256,256]{1,0:T(8,128)S(1)}, u32[]{:S(2)}, u32[]{:S(2)}) collective-permute-start(f32[256,256]{1,0:T(8,128)S(1)} %collective-permute-done.1.right_imag), channel_id=1, source_target_pairs={{16,0},{32,16},{48,32},{64,48},{80,64},{96,80},{112,96},{128,112},... | collective-permute-start | bytes 786440 | tf_op jit(solution)/shard_map/ppermute | solution.py:22
  21.7 2.4 %collective-permute-done.3.corner_real = f32[256,256]{1,0:T(8,128)S(1)} collective-permute-done((f32[256,256]{1,0:T(8,128)S(1)}, f32[256,256]{1,0:T(8,128)S(1)}, u32[]{:S(2)}, u32[]{:S(2)}) %collective-permute-start.3) | collective-permute-done | bytes 262176 | tf_op jit(solution)/shard_map/ppermute | solution.py:22
  24.1 4.0 %collective-permute-done.4.corner_imag = f32[256,256]{1,0:T(8,128)S(1)} collective-permute-done((f32[256,256]{1,0:T(8,128)S(1)}, f32[256,256]{1,0:T(8,128)S(1)}, u32[]{:S(2)}, u32[]{:S(2)}) %collective-permute-start.4) | collective-permute-done | bytes 262176 | tf_op jit(solution)/shard_map/ppermute | solution.py:22
  28.1 5.9 %shard_map.69 = (f32[32,3,8,128]{3,2,1,0:T(8,128)S(1)}, f32[32,3,8,128]{3,2,1,0:T(8,128)S(1)}, f32[2,256,256]{2,1,0:T(8,128)S(1)}, f32[2,256,256]{2,1,0:T(8,128)S(1)}, f32[2,2,256,256]{3,2,1,0:T(8,128)S(1)}) custom-call(s32[2,2]{1,0:T(2,128)S(1)} %bitcast.21, s32[1]{0:T(128)} %bitcast.1.core, f32[2,256,256]{2,1,0:T(8,128)S(1)} %copy-done.1, ...), custom_call_target="tpu_custom_call" | custom-call | flops 3221225472 | bytes 8388608 | tf_op jit(solution)/shard_map/pallas_call | solution.py:228
  34.0 1.9 %collective-permute-start.5 = (f32[32,3,8,128]{3,2,1,0:T(8,128)S(1)}, f32[32,3,8,128]{3,2,1,0:T(8,128)S(1)}, u32[]{:S(2)}, u32[]{:S(2)}) collective-permute-start(f32[32,3,8,128]{3,2,1,0:T(8,128)S(1)} %get-tuple-element.19), channel_id=1, source_target_pairs={{0,16},{16,0},{1,17},{17,1},{2,18},{18,2},{3,19},{19,3},{4,20},{20... | collective-permute-start | bytes 1179656 | tf_op jit(solution)/shard_map/ppermute | solution.py:290
  36.0 1.7 %collective-permute-done.5 = f32[32,3,8,128]{3,2,1,0:T(8,128)S(1)} collective-permute-done((f32[32,3,8,128]{3,2,1,0:T(8,128)S(1)}, f32[32,3,8,128]{3,2,1,0:T(8,128)S(1)}, u32[]{:S(2)}, u32[]{:S(2)}) %collective-permute-start.5) | collective-permute-done | bytes 393248 | tf_op jit(solution)/shard_map/ppermute | solution.py:290
  37.6 0.8 add_bitcast_fusion
  38.4 17.0 %all-to-all-start = ((f32[32,24,128]{2,1,0:T(8,128)}), f32[32,24,128]{2,1,0:T(8,128)S(1)}, u32[]{:S(2)}, u32[]{:S(2)}) async-start(f32[32,24,128]{2,1,0:T(8,128)} %add_bitcast_fusion), calls=%async_computation | async-start | bytes 786432 | tf_op jit(solution)/shard_map/all_to_all | solution.py:294
  55.4 5.2 %collective-permute-start.6 = (f32[2,2,256,256]{3,2,1,0:T(8,128)}, f32[2,2,256,256]{3,2,1,0:T(8,128)S(1)}, u32[]{:S(2)}, u32[]{:S(2)}) collective-permute-start(f32[2,2,256,256]{3,2,1,0:T(8,128)} %copy-done.4), channel_id=1, source_target_pairs={{0,16},{16,32},{32,48},{48,64},{64,80},{80,96},{96,112},{112,128},... | collective-permute-start | bytes 3145736 | tf_op jit(solution)/shard_map/ppermute | solution.py:22
  60.7 6.9 %all-to-all-done.parts = f32[32,24,128]{2,1,0:T(8,128)S(1)} async-done(((f32[32,24,128]{2,1,0:T(8,128)}), f32[32,24,128]{2,1,0:T(8,128)S(1)}, u32[]{:S(2)}, u32[]{:S(2)}) %all-to-all-start) | async-done | bytes 393248 | tf_op jit(solution)/shard_map/all_to_all | solution.py:294
  67.6 0.0 copy-start.2
  67.6 0.6 copy-done.2
  68.3 7.3 %all-to-all-start.1 = ((f32[8,24,128]{2,1,0:T(8,128)}), f32[8,24,128]{2,1,0:T(8,128)S(1)}, u32[]{:S(2)}, u32[]{:S(2)}) async-start(f32[8,24,128]{2,1,0:T(8,128)} %copy-done.2), calls=%async_computation.1 | async-start | bytes 196608 | tf_op jit(solution)/shard_map/all_to_all | solution.py:296
  75.5 0.9 fusion
  76.4 4.3 %collective-permute-start.7 = (f32[2,256,256]{2,1,0:T(8,128)}, f32[2,256,256]{2,1,0:T(8,128)S(1)}, u32[]{:S(2)}, u32[]{:S(2)}) collective-permute-start(f32[2,256,256]{2,1,0:T(8,128)} %fusion), channel_id=1, source_target_pairs={{0,1},{1,2},{2,3},{3,4},{4,5},{5,6},{6,7},{7,8},{8,9},{9,10},{10,1... | collective-permute-start | bytes 1572872 | tf_op jit(solution)/shard_map/ppermute | solution.py:22
  80.7 2.4 %all-to-all-done.1.parts = f32[8,24,128]{2,1,0:T(8,128)S(1)} async-done(((f32[8,24,128]{2,1,0:T(8,128)}), f32[8,24,128]{2,1,0:T(8,128)S(1)}, u32[]{:S(2)}, u32[]{:S(2)}) %all-to-all-start.1) | async-done | bytes 98336 | tf_op jit(solution)/shard_map/all_to_all | solution.py:296
  83.1 0.7 shard_map.71
  83.8 7.0 %all-to-all-start.2 = ((f32[32,16,128]{2,1,0:T(8,128)}), f32[32,16,128]{2,1,0:T(8,128)S(1)}, u32[]{:S(2)}, u32[]{:S(2)}) async-start(f32[32,16,128]{2,1,0:T(8,128)} %shard_map.71), calls=%async_computation.2 | async-start | bytes 524288 | tf_op jit(solution)/shard_map/all_to_all | solution.py:299
  90.9 2.5 %shard_map.72 = f32[2,256,256]{2,1,0:T(8,128)} custom-call(s32[2,2]{1,0:T(2,128)S(1)} %bitcast.22, f32[2,256,256]{2,1,0:T(8,128)S(1)} %copy-done, f32[2,256,256]{2,1,0:T(8,128)S(1)} %copy-done.1, f32[2,256,256]{2,1,0:T(8,128)S(1)} %get-tuple-element.25.step_own, f32[2,2,256,256]{3,2,1,0:T(8,128)S(1)} %collective-permute-done.6.step_row, ...), custom_call_target="tpu_custom_call" | custom-call | flops 8000000 | bytes 8388608 | tf_op jit(solution)/shard_map/pallas_call | solution.py:209
  93.3 7.2 %all-to-all-done.2 = f32[32,16,128]{2,1,0:T(8,128)S(1)} async-done(((f32[32,16,128]{2,1,0:T(8,128)}), f32[32,16,128]{2,1,0:T(8,128)S(1)}, u32[]{:S(2)}, u32[]{:S(2)}) %all-to-all-start.2) | async-done | bytes 262176 | tf_op jit(solution)/shard_map/all_to_all | solution.py:299
  100.5 6.1 %collective-permute-start.8 = (f32[32,16,128]{2,1,0:T(8,128)S(1)}, f32[32,16,128]{2,1,0:T(8,128)S(1)}, u32[]{:S(2)}, u32[]{:S(2)}) collective-permute-start(f32[32,16,128]{2,1,0:T(8,128)S(1)} %all-to-all-done.2), channel_id=1, source_target_pairs={{0,16},{16,0},{1,17},{17,1},{2,18},{18,2},{3,19},{19,3},{4,20},{20... | collective-permute-start | bytes 786440 | tf_op jit(solution)/shard_map/ppermute | solution.py:302
  106.6 1.1 %collective-permute-done.8 = f32[32,16,128]{2,1,0:T(8,128)S(1)} collective-permute-done((f32[32,16,128]{2,1,0:T(8,128)S(1)}, f32[32,16,128]{2,1,0:T(8,128)S(1)}, u32[]{:S(2)}, u32[]{:S(2)}) %collective-permute-start.8) | collective-permute-done | bytes 262176 | tf_op jit(solution)/shard_map/ppermute | solution.py:302
  107.8 0.8 copy_bitcast_fusion
  (16 shorter events, 0.1 us)
Async XLA Ops:
  0.6 3.8 %copy-start.1 = (f32[2,256,256]{2,1,0:T(8,128)S(1)}, f32[2,256,256]{2,1,0:T(8,128)}, u32[]{:S(2)}) copy-start(f32[2,256,256]{2,1,0:T(8,128)} %tile.3) | copy-start | bytes 1572868
  0.6 12.6 %copy-start = (f32[2,256,256]{2,1,0:T(8,128)S(1)}, f32[2,256,256]{2,1,0:T(8,128)}, u32[]{:S(2)}) copy-start(f32[2,256,256]{2,1,0:T(8,128)} %probe.3) | copy-start | bytes 1572868
  1.8 13.1 %collective-permute-start = (f32[256,256]{1,0:T(8,128)S(1)}, f32[256,256]{1,0:T(8,128)S(1)}, u32[]{:S(2)}, u32[]{:S(2)}) collective-permute-start(f32[256,256]{1,0:T(8,128)S(1)} %get-tuple-element.31), channel_id=1, source_target_pairs={{1,0},{2,1},{3,2},{4,3},{5,4},{6,5},{7,6},{8,7},{9,8},{10,9},{11,1... | collective-permute-start | bytes 786440 | tf_op jit(solution)/shard_map/ppermute | solution.py:22
  3.1 15.8 %collective-permute-start.1 = (f32[256,256]{1,0:T(8,128)S(1)}, f32[256,256]{1,0:T(8,128)S(1)}, u32[]{:S(2)}, u32[]{:S(2)}) collective-permute-start(f32[256,256]{1,0:T(8,128)S(1)} %get-tuple-element.30), channel_id=1, source_target_pairs={{1,0},{2,1},{3,2},{4,3},{5,4},{6,5},{7,6},{8,7},{9,8},{10,9},{11,1... | collective-permute-start | bytes 786440 | tf_op jit(solution)/shard_map/ppermute | solution.py:22
  4.4 23.7 %collective-permute-start.2 = (f32[2,256,256]{2,1,0:T(8,128)S(1)}, f32[2,256,256]{2,1,0:T(8,128)S(1)}, u32[]{:S(2)}, u32[]{:S(2)}) collective-permute-start(f32[2,256,256]{2,1,0:T(8,128)S(1)} %copy-done.1), channel_id=1, source_target_pairs={{16,0},{32,16},{48,32},{64,48},{80,64},{96,80},{112,96},{128,112},... | collective-permute-start | bytes 1572872 | tf_op jit(solution)/shard_map/ppermute | solution.py:22
  13.2 0.7 copy-start.3
  13.9 14.2 %copy-start.5 = (bf16[1,1,2,256,256]{4,3,2,1,0:T(8,128)(2,1)S(1)}, bf16[1,1,2,256,256]{4,3,2,1,0:T(8,128)(2,1)}, u32[]{:S(2)}) copy-start(bf16[1,1,2,256,256]{4,3,2,1,0:T(8,128)(2,1)} %param.6) | copy-start | bytes 786436
  13.9 14.2 %copy-start.6 = (bf16[3,2,256,256]{3,2,1,0:T(8,128)(2,1)S(1)}, bf16[3,2,256,256]{3,2,1,0:T(8,128)(2,1)}, u32[]{:S(2)}) copy-start(bf16[3,2,256,256]{3,2,1,0:T(8,128)(2,1)} %constant.29.clone.tables) | copy-start | bytes 2359300
  14.9 9.2 %collective-permute-start.3 = (f32[256,256]{1,0:T(8,128)S(1)}, f32[256,256]{1,0:T(8,128)S(1)}, u32[]{:S(2)}, u32[]{:S(2)}) collective-permute-start(f32[256,256]{1,0:T(8,128)S(1)} %collective-permute-done.right_real), channel_id=1, source_target_pairs={{16,0},{32,16},{48,32},{64,48},{80,64},{96,80},{112,96},{128,112},... | collective-permute-start | bytes 786440 | tf_op jit(solution)/shard_map/ppermute | solution.py:22
  18.9 9.2 %collective-permute-start.4 = (f32[256,256]{1,0:T(8,128)S(1)}, f32[256,256]{1,0:T(8,128)S(1)}, u32[]{:S(2)}, u32[]{:S(2)}) collective-permute-start(f32[256,256]{1,0:T(8,128)S(1)} %collective-permute-done.1.right_imag), channel_id=1, source_target_pairs={{16,0},{32,16},{48,32},{64,48},{80,64},{96,80},{112,96},{128,112},... | collective-permute-start | bytes 786440 | tf_op jit(solution)/shard_map/ppermute | solution.py:22
  34.0 4.4 %copy-start.4 = (f32[2,2,256,256]{3,2,1,0:T(8,128)}, f32[2,2,256,256]{3,2,1,0:T(8,128)S(1)}, u32[]{:S(2)}) copy-start(f32[2,2,256,256]{3,2,1,0:T(8,128)S(1)} %get-tuple-element.22) | copy-start | bytes 3145732
  34.0 3.6 %collective-permute-start.5 = (f32[32,3,8,128]{3,2,1,0:T(8,128)S(1)}, f32[32,3,8,128]{3,2,1,0:T(8,128)S(1)}, u32[]{:S(2)}, u32[]{:S(2)}) collective-permute-start(f32[32,3,8,128]{3,2,1,0:T(8,128)S(1)} %get-tuple-element.19), channel_id=1, source_target_pairs={{0,16},{16,0},{1,17},{17,1},{2,18},{18,2},{3,19},{19,3},{4,20},{20... | collective-permute-start | bytes 1179656 | tf_op jit(solution)/shard_map/ppermute | solution.py:290
  38.4 29.1 %all-to-all-start = ((f32[32,24,128]{2,1,0:T(8,128)}), f32[32,24,128]{2,1,0:T(8,128)S(1)}, u32[]{:S(2)}, u32[]{:S(2)}) async-start(f32[32,24,128]{2,1,0:T(8,128)} %add_bitcast_fusion), calls=%async_computation | async-start | bytes 786432 | tf_op jit(solution)/shard_map/all_to_all | solution.py:294
  55.4 20.1 %collective-permute-start.6 = (f32[2,2,256,256]{3,2,1,0:T(8,128)}, f32[2,2,256,256]{3,2,1,0:T(8,128)S(1)}, u32[]{:S(2)}, u32[]{:S(2)}) collective-permute-start(f32[2,2,256,256]{3,2,1,0:T(8,128)} %copy-done.4), channel_id=1, source_target_pairs={{0,16},{16,32},{32,48},{48,64},{64,80},{80,96},{96,112},{112,128},... | collective-permute-start | bytes 3145736 | tf_op jit(solution)/shard_map/ppermute | solution.py:22
  67.6 0.6 copy-start.2
  68.3 14.8 %all-to-all-start.1 = ((f32[8,24,128]{2,1,0:T(8,128)}), f32[8,24,128]{2,1,0:T(8,128)S(1)}, u32[]{:S(2)}, u32[]{:S(2)}) async-start(f32[8,24,128]{2,1,0:T(8,128)} %copy-done.2), calls=%async_computation.1 | async-start | bytes 196608 | tf_op jit(solution)/shard_map/all_to_all | solution.py:296
  76.4 14.5 %collective-permute-start.7 = (f32[2,256,256]{2,1,0:T(8,128)}, f32[2,256,256]{2,1,0:T(8,128)S(1)}, u32[]{:S(2)}, u32[]{:S(2)}) collective-permute-start(f32[2,256,256]{2,1,0:T(8,128)} %fusion), channel_id=1, source_target_pairs={{0,1},{1,2},{2,3},{3,4},{4,5},{5,6},{6,7},{7,8},{8,9},{9,10},{10,1... | collective-permute-start | bytes 1572872 | tf_op jit(solution)/shard_map/ppermute | solution.py:22
  83.8 16.7 %all-to-all-start.2 = ((f32[32,16,128]{2,1,0:T(8,128)}), f32[32,16,128]{2,1,0:T(8,128)S(1)}, u32[]{:S(2)}, u32[]{:S(2)}) async-start(f32[32,16,128]{2,1,0:T(8,128)} %shard_map.71), calls=%async_computation.2 | async-start | bytes 524288 | tf_op jit(solution)/shard_map/all_to_all | solution.py:299
  100.5 7.3 %collective-permute-start.8 = (f32[32,16,128]{2,1,0:T(8,128)S(1)}, f32[32,16,128]{2,1,0:T(8,128)S(1)}, u32[]{:S(2)}, u32[]{:S(2)}) collective-permute-start(f32[32,16,128]{2,1,0:T(8,128)S(1)} %all-to-all-done.2), channel_id=1, source_target_pairs={{0,16},{16,0},{1,17},{17,1},{2,18},{18,2},{3,19},{19,3},{4,20},{20... | collective-permute-start | bytes 786440 | tf_op jit(solution)/shard_map/ppermute | solution.py:302

commit v5 on v4

--- a/solution.py
+++ b/solution.py
@@ -13,7 +13,7 @@
 SIDE = 256
 ROW = ("y", "xh", "c")
 COL = ("xl", "z")
-PLANE = ("xh", "xl", "z")
+PLANE = ("xl", "xh", "z")
 
 
 def passed_along(value, axis, steps):
@@ -277,7 +277,7 @@
     core = lax.axis_index("c")
     corner = lax.dynamic_slice(probe, (0, lax.axis_index(PLANE) * 8, core * (SIDE // 2)), (2, 8, SIDE // 2))
     right_real = passed_along(object_field[0], COL, -1)
-    right_imag = passed_along(object_field[1], COL, -1)
+    right_imag = passed_along(lax.optimization_barrier(object_field)[1], COL, -1)
     below_tile = passed_along(object_field, ROW, -1)
     rolled_probe = prepare(own, probe)
     right_real, rolled_probe, corner = lax.optimization_barrier((right_real, rolled_probe, corner))

time: 109 us -> 109 us (level)
  starting transfers between devices: 67 us -> 65.8 us
    all_to_all x1, starting transfers between devices: 7 us -> 5.82 us  [body(): near = lax.all_to_all(settle(summed, corner, rows), PLANE, 0, 0)]
  transfers between devices with their start and end apart: 12 -> 12, of which waited for: 7 -> 8; matrix products, arithmetic and copies ran while one was open for 1% -> 1% of each run, Pallas kernels for 4% -> 4%
where the time goes in v5:
time: 109 us; the launch traced here: 108 us
  starting transfers between devices  65.8 us (60%)
  waiting for transfers between devices  26.5 us (24%)
  Pallas kernels  10.1 us (9%)
  other arithmetic  2.48 us (2%)
  local copies, waits for them, and re-layouts  2.41 us (2%)
    ppermute x7, starting transfers between devices, passed_along(): lax.ppermute(value, axis, [(source, source + steps) for source in range(l...  27.8 us
    all_to_all x1, starting transfers between devices, body(): summed = lax.all_to_all(pair, PLANE, 0, 0)  16.9 us
    all_to_all x1, starting transfers between devices, body(): summed = lax.all_to_all(fold(summed, lax.axis_size('y')), 'y', 0, 0)  7.43 us
    all_to_all x1, waiting for transfers between devices, body(): summed = lax.all_to_all(pair, PLANE, 0, 0)  7.38 us
    ppermute x7, waiting for transfers between devices, passed_along(): lax.ppermute(value, axis, [(source, source + steps) for source in range(l...  7.06 us
    all_to_all x1, waiting for transfers between devices, body(): near = lax.all_to_all(settle(summed, corner, rows), PLANE, 0, 0)  6.88 us
    pallas_call x1, Pallas kernels, visit(): pl.pallas_call(visit_kernel, out_shape=out_shape, in_specs=[smem(), smem(...  5.91 us
    ppermute x1, starting transfers between devices, body(): far = lax.ppermute(near, 'c', [(0, 1), (1, 0)])  5.89 us
  transfers between devices with their start and end apart: 12, of which 8 were waited for; matrix products, arithmetic and copies ran while one was open for 1% of the time, Pallas kernels for 4%

profile of v5, /device:TPU:1, one launch (start us, length us, event | category | flops | bytes accessed | tf_op | source)
XLA Modules:
  0.0 108.1 jit_solution(10230759568840847695)
XLA Ops:
  0.6 1.1 slice_bitcast_fusion.2
  1.7 1.3 %collective-permute-start = (f32[256,256]{1,0:T(8,128)S(1)}, f32[256,256]{1,0:T(8,128)S(1)}, u32[]{:S(2)}, u32[]{:S(2)}) collective-permute-start(f32[256,256]{1,0:T(8,128)S(1)} %slice_bitcast_fusion.2), channel_id=1, source_target_pairs={{1,0},{2,1},{3,2},{4,3},{5,4},{6,5},{7,6},{8,7},{9,8},{10,9},{11,1... | collective-permute-start | bytes 786440 | tf_op jit(solution)/shard_map/ppermute | solution.py:22
  3.0 1.3 %collective-permute-start.1 = (f32[256,256]{1,0:T(8,128)S(1)}, f32[256,256]{1,0:T(8,128)S(1)}, u32[]{:S(2)}, u32[]{:S(2)}) collective-permute-start(f32[256,256]{1,0:T(8,128)S(1)} %slice_bitcast_fusion.1), channel_id=1, source_target_pairs={{1,0},{2,1},{3,2},{4,3},{5,4},{6,5},{7,6},{8,7},{9,8},{10,9},{11,1... | collective-permute-start | bytes 786440 | tf_op jit(solution)/shard_map/ppermute | solution.py:22
  4.3 8.8 %collective-permute-start.2 = (f32[2,256,256]{2,1,0:T(8,128)S(1)}, f32[2,256,256]{2,1,0:T(8,128)S(1)}, u32[]{:S(2)}, u32[]{:S(2)}) collective-permute-start(f32[2,256,256]{2,1,0:T(8,128)S(1)} %copy-done.1), channel_id=1, source_target_pairs={{16,0},{32,16},{48,32},{64,48},{80,64},{96,80},{112,96},{128,112},... | collective-permute-start | bytes 1572872 | tf_op jit(solution)/shard_map/ppermute | solution.py:22
  13.1 0.0 copy-start.3
  13.2 0.7 copy-done.3
  13.8 0.9 shard_map.68.rolled_probe
  14.8 3.9 %collective-permute-start.3 = (f32[256,256]{1,0:T(8,128)S(1)}, f32[256,256]{1,0:T(8,128)S(1)}, u32[]{:S(2)}, u32[]{:S(2)}) collective-permute-start(f32[256,256]{1,0:T(8,128)S(1)} %collective-permute-done.right_real), channel_id=1, source_target_pairs={{16,0},{32,16},{48,32},{64,48},{80,64},{96,80},{112,96},{128,112},... | collective-permute-start | bytes 786440 | tf_op jit(solution)/shard_map/ppermute | solution.py:22
  18.8 2.8 %collective-permute-start.4 = (f32[256,256]{1,0:T(8,128)S(1)}, f32[256,256]{1,0:T(8,128)S(1)}, u32[]{:S(2)}, u32[]{:S(2)}) collective-permute-start(f32[256,256]{1,0:T(8,128)S(1)} %collective-permute-done.1.right_imag), channel_id=1, source_target_pairs={{16,0},{32,16},{48,32},{64,48},{80,64},{96,80},{112,96},{128,112},... | collective-permute-start | bytes 786440 | tf_op jit(solution)/shard_map/ppermute | solution.py:22
  21.6 2.5 %collective-permute-done.3.corner_real = f32[256,256]{1,0:T(8,128)S(1)} collective-permute-done((f32[256,256]{1,0:T(8,128)S(1)}, f32[256,256]{1,0:T(8,128)S(1)}, u32[]{:S(2)}, u32[]{:S(2)}) %collective-permute-start.3) | collective-permute-done | bytes 262176 | tf_op jit(solution)/shard_map/ppermute | solution.py:22
  24.0 4.0 %collective-permute-done.4.corner_imag = f32[256,256]{1,0:T(8,128)S(1)} collective-permute-done((f32[256,256]{1,0:T(8,128)S(1)}, f32[256,256]{1,0:T(8,128)S(1)}, u32[]{:S(2)}, u32[]{:S(2)}) %collective-permute-start.4) | collective-permute-done | bytes 262176 | tf_op jit(solution)/shard_map/ppermute | solution.py:22
  28.0 5.9 %shard_map.69 = (f32[32,3,8,128]{3,2,1,0:T(8,128)S(1)}, f32[32,3,8,128]{3,2,1,0:T(8,128)S(1)}, f32[2,256,256]{2,1,0:T(8,128)S(1)}, f32[2,256,256]{2,1,0:T(8,128)S(1)}, f32[2,2,256,256]{3,2,1,0:T(8,128)S(1)}) custom-call(s32[2,2]{1,0:T(2,128)S(1)} %bitcast.21, s32[1]{0:T(128)} %bitcast.1.core, f32[2,256,256]{2,1,0:T(8,128)S(1)} %copy-done.1, ...), custom_call_target="tpu_custom_call" | custom-call | flops 3221225472 | bytes 8388608 | tf_op jit(solution)/shard_map/pallas_call | solution.py:228
  33.9 1.9 %collective-permute-start.5 = (f32[32,3,8,128]{3,2,1,0:T(8,128)S(1)}, f32[32,3,8,128]{3,2,1,0:T(8,128)S(1)}, u32[]{:S(2)}, u32[]{:S(2)}) collective-permute-start(f32[32,3,8,128]{3,2,1,0:T(8,128)S(1)} %get-tuple-element.19), channel_id=1, source_target_pairs={{0,16},{16,0},{1,17},{17,1},{2,18},{18,2},{3,19},{19,3},{4,20},{20... | collective-permute-start | bytes 1179656 | tf_op jit(solution)/shard_map/ppermute | solution.py:290
  35.9 1.7 %collective-permute-done.5 = f32[32,3,8,128]{3,2,1,0:T(8,128)S(1)} collective-permute-done((f32[32,3,8,128]{3,2,1,0:T(8,128)S(1)}, f32[32,3,8,128]{3,2,1,0:T(8,128)S(1)}, u32[]{:S(2)}, u32[]{:S(2)}) %collective-permute-start.5) | collective-permute-done | bytes 393248 | tf_op jit(solution)/shard_map/ppermute | solution.py:290
  37.5 0.8 add_bitcast_fusion
  38.3 16.9 %all-to-all-start = ((f32[32,24,128]{2,1,0:T(8,128)}), f32[32,24,128]{2,1,0:T(8,128)S(1)}, u32[]{:S(2)}, u32[]{:S(2)}) async-start(f32[32,24,128]{2,1,0:T(8,128)} %add_bitcast_fusion), calls=%async_computation | async-start | bytes 786432 | tf_op jit(solution)/shard_map/all_to_all | solution.py:294
  55.3 5.2 %collective-permute-start.6 = (f32[2,2,256,256]{3,2,1,0:T(8,128)}, f32[2,2,256,256]{3,2,1,0:T(8,128)S(1)}, u32[]{:S(2)}, u32[]{:S(2)}) collective-permute-start(f32[2,2,256,256]{3,2,1,0:T(8,128)} %copy-done.4), channel_id=1, source_target_pairs={{0,16},{16,32},{32,48},{48,64},{64,80},{80,96},{96,112},{112,128},... | collective-permute-start | bytes 3145736 | tf_op jit(solution)/shard_map/ppermute | solution.py:22
  60.5 7.4 %all-to-all-done.parts = f32[32,24,128]{2,1,0:T(8,128)S(1)} async-done(((f32[32,24,128]{2,1,0:T(8,128)}), f32[32,24,128]{2,1,0:T(8,128)S(1)}, u32[]{:S(2)}, u32[]{:S(2)}) %all-to-all-start) | async-done | bytes 393248 | tf_op jit(solution)/shard_map/all_to_all | solution.py:294
  68.0 0.0 copy-start.2
  68.0 0.6 copy-done.2
  68.6 7.4 %all-to-all-start.1 = ((f32[8,24,128]{2,1,0:T(8,128)}), f32[8,24,128]{2,1,0:T(8,128)S(1)}, u32[]{:S(2)}, u32[]{:S(2)}) async-start(f32[8,24,128]{2,1,0:T(8,128)} %copy-done.2), calls=%async_computation.1 | async-start | bytes 196608 | tf_op jit(solution)/shard_map/all_to_all | solution.py:296
  76.0 0.9 fusion
  76.9 4.5 %collective-permute-start.7 = (f32[2,256,256]{2,1,0:T(8,128)}, f32[2,256,256]{2,1,0:T(8,128)S(1)}, u32[]{:S(2)}, u32[]{:S(2)}) collective-permute-start(f32[2,256,256]{2,1,0:T(8,128)} %fusion), channel_id=1, source_target_pairs={{0,1},{1,2},{2,3},{3,4},{4,5},{5,6},{6,7},{7,8},{8,9},{9,10},{10,1... | collective-permute-start | bytes 1572872 | tf_op jit(solution)/shard_map/ppermute | solution.py:22
  81.4 2.3 %all-to-all-done.1.parts = f32[8,24,128]{2,1,0:T(8,128)S(1)} async-done(((f32[8,24,128]{2,1,0:T(8,128)}), f32[8,24,128]{2,1,0:T(8,128)S(1)}, u32[]{:S(2)}, u32[]{:S(2)}) %all-to-all-start.1) | async-done | bytes 98336 | tf_op jit(solution)/shard_map/all_to_all | solution.py:296
  83.7 0.7 shard_map.71
  84.5 5.8 %all-to-all-start.2 = ((f32[32,16,128]{2,1,0:T(8,128)}), f32[32,16,128]{2,1,0:T(8,128)S(1)}, u32[]{:S(2)}, u32[]{:S(2)}) async-start(f32[32,16,128]{2,1,0:T(8,128)} %shard_map.71), calls=%async_computation.2 | async-start | bytes 524288 | tf_op jit(solution)/shard_map/all_to_all | solution.py:299
  90.3 0.6 collective-permute-done.7.step_right
  90.9 2.5 %shard_map.72 = f32[2,256,256]{2,1,0:T(8,128)} custom-call(s32[2,2]{1,0:T(2,128)S(1)} %bitcast.22, f32[2,256,256]{2,1,0:T(8,128)S(1)} %copy-done, f32[2,256,256]{2,1,0:T(8,128)S(1)} %copy-done.1, f32[2,256,256]{2,1,0:T(8,128)S(1)} %get-tuple-element.25.step_own, f32[2,2,256,256]{3,2,1,0:T(8,128)S(1)} %collective-permute-done.6.step_row, ...), custom_call_target="tpu_custom_call" | custom-call | flops 8000000 | bytes 8388608 | tf_op jit(solution)/shard_map/pallas_call | solution.py:209
  93.4 6.9 %all-to-all-done.2 = f32[32,16,128]{2,1,0:T(8,128)S(1)} async-done(((f32[32,16,128]{2,1,0:T(8,128)}), f32[32,16,128]{2,1,0:T(8,128)S(1)}, u32[]{:S(2)}, u32[]{:S(2)}) %all-to-all-start.2) | async-done | bytes 262176 | tf_op jit(solution)/shard_map/all_to_all | solution.py:299
  100.3 5.9 %collective-permute-start.8 = (f32[32,16,128]{2,1,0:T(8,128)S(1)}, f32[32,16,128]{2,1,0:T(8,128)S(1)}, u32[]{:S(2)}, u32[]{:S(2)}) collective-permute-start(f32[32,16,128]{2,1,0:T(8,128)S(1)} %all-to-all-done.2), channel_id=1, source_target_pairs={{0,16},{16,0},{1,17},{17,1},{2,18},{18,2},{3,19},{19,3},{4,20},{20... | collective-permute-start | bytes 786440 | tf_op jit(solution)/shard_map/ppermute | solution.py:302
  106.2 1.1 %collective-permute-done.8 = f32[32,16,128]{2,1,0:T(8,128)S(1)} collective-permute-done((f32[32,16,128]{2,1,0:T(8,128)S(1)}, f32[32,16,128]{2,1,0:T(8,128)S(1)}, u32[]{:S(2)}, u32[]{:S(2)}) %collective-permute-start.8) | collective-permute-done | bytes 262176 | tf_op jit(solution)/shard_map/ppermute | solution.py:302
  107.3 0.8 copy_bitcast_fusion
  (17 shorter events, 0.1 us)
Async XLA Ops:
  0.6 2.4 %copy-start.1 = (f32[2,256,256]{2,1,0:T(8,128)S(1)}, f32[2,256,256]{2,1,0:T(8,128)}, u32[]{:S(2)}) copy-start(f32[2,256,256]{2,1,0:T(8,128)} %tile.3) | copy-start | bytes 1572868
  0.6 12.5 %copy-start = (f32[2,256,256]{2,1,0:T(8,128)S(1)}, f32[2,256,256]{2,1,0:T(8,128)}, u32[]{:S(2)}) copy-start(f32[2,256,256]{2,1,0:T(8,128)} %probe.3) | copy-start | bytes 1572868
  1.7 13.1 %collective-permute-start = (f32[256,256]{1,0:T(8,128)S(1)}, f32[256,256]{1,0:T(8,128)S(1)}, u32[]{:S(2)}, u32[]{:S(2)}) collective-permute-start(f32[256,256]{1,0:T(8,128)S(1)} %slice_bitcast_fusion.2), channel_id=1, source_target_pairs={{1,0},{2,1},{3,2},{4,3},{5,4},{6,5},{7,6},{8,7},{9,8},{10,9},{11,1... | collective-permute-start | bytes 786440 | tf_op jit(solution)/shard_map/ppermute | solution.py:22
  3.0 15.7 %collective-permute-start.1 = (f32[256,256]{1,0:T(8,128)S(1)}, f32[256,256]{1,0:T(8,128)S(1)}, u32[]{:S(2)}, u32[]{:S(2)}) collective-permute-start(f32[256,256]{1,0:T(8,128)S(1)} %slice_bitcast_fusion.1), channel_id=1, source_target_pairs={{1,0},{2,1},{3,2},{4,3},{5,4},{6,5},{7,6},{8,7},{9,8},{10,9},{11,1... | collective-permute-start | bytes 786440 | tf_op jit(solution)/shard_map/ppermute | solution.py:22
  4.3 23.6 %collective-permute-start.2 = (f32[2,256,256]{2,1,0:T(8,128)S(1)}, f32[2,256,256]{2,1,0:T(8,128)S(1)}, u32[]{:S(2)}, u32[]{:S(2)}) collective-permute-start(f32[2,256,256]{2,1,0:T(8,128)S(1)} %copy-done.1), channel_id=1, source_target_pairs={{16,0},{32,16},{48,32},{64,48},{80,64},{96,80},{112,96},{128,112},... | collective-permute-start | bytes 1572872 | tf_op jit(solution)/shard_map/ppermute | solution.py:22
  13.1 0.7 copy-start.3
  13.8 14.2 %copy-start.5 = (bf16[1,1,2,256,256]{4,3,2,1,0:T(8,128)(2,1)S(1)}, bf16[1,1,2,256,256]{4,3,2,1,0:T(8,128)(2,1)}, u32[]{:S(2)}) copy-start(bf16[1,1,2,256,256]{4,3,2,1,0:T(8,128)(2,1)} %param.6) | copy-start | bytes 786436
  13.8 14.2 %copy-start.6 = (bf16[3,2,256,256]{3,2,1,0:T(8,128)(2,1)S(1)}, bf16[3,2,256,256]{3,2,1,0:T(8,128)(2,1)}, u32[]{:S(2)}) copy-start(bf16[3,2,256,256]{3,2,1,0:T(8,128)(2,1)} %constant.29.clone.tables) | copy-start | bytes 2359300
  14.8 9.2 %collective-permute-start.3 = (f32[256,256]{1,0:T(8,128)S(1)}, f32[256,256]{1,0:T(8,128)S(1)}, u32[]{:S(2)}, u32[]{:S(2)}) collective-permute-start(f32[256,256]{1,0:T(8,128)S(1)} %collective-permute-done.right_real), channel_id=1, source_target_pairs={{16,0},{32,16},{48,32},{64,48},{80,64},{96,80},{112,96},{128,112},... | collective-permute-start | bytes 786440 | tf_op jit(solution)/shard_map/ppermute | solution.py:22
  18.8 9.2 %collective-permute-start.4 = (f32[256,256]{1,0:T(8,128)S(1)}, f32[256,256]{1,0:T(8,128)S(1)}, u32[]{:S(2)}, u32[]{:S(2)}) collective-permute-start(f32[256,256]{1,0:T(8,128)S(1)} %collective-permute-done.1.right_imag), channel_id=1, source_target_pairs={{16,0},{32,16},{48,32},{64,48},{80,64},{96,80},{112,96},{128,112},... | collective-permute-start | bytes 786440 | tf_op jit(solution)/shard_map/ppermute | solution.py:22
  33.9 4.4 %copy-start.4 = (f32[2,2,256,256]{3,2,1,0:T(8,128)}, f32[2,2,256,256]{3,2,1,0:T(8,128)S(1)}, u32[]{:S(2)}) copy-start(f32[2,2,256,256]{3,2,1,0:T(8,128)S(1)} %get-tuple-element.22) | copy-start | bytes 3145732
  33.9 3.6 %collective-permute-start.5 = (f32[32,3,8,128]{3,2,1,0:T(8,128)S(1)}, f32[32,3,8,128]{3,2,1,0:T(8,128)S(1)}, u32[]{:S(2)}, u32[]{:S(2)}) collective-permute-start(f32[32,3,8,128]{3,2,1,0:T(8,128)S(1)} %get-tuple-element.19), channel_id=1, source_target_pairs={{0,16},{16,0},{1,17},{17,1},{2,18},{18,2},{3,19},{19,3},{4,20},{20... | collective-permute-start | bytes 1179656 | tf_op jit(solution)/shard_map/ppermute | solution.py:290
  38.3 29.6 %all-to-all-start = ((f32[32,24,128]{2,1,0:T(8,128)}), f32[32,24,128]{2,1,0:T(8,128)S(1)}, u32[]{:S(2)}, u32[]{:S(2)}) async-start(f32[32,24,128]{2,1,0:T(8,128)} %add_bitcast_fusion), calls=%async_computation | async-start | bytes 786432 | tf_op jit(solution)/shard_map/all_to_all | solution.py:294
  55.3 20.8 %collective-permute-start.6 = (f32[2,2,256,256]{3,2,1,0:T(8,128)}, f32[2,2,256,256]{3,2,1,0:T(8,128)S(1)}, u32[]{:S(2)}, u32[]{:S(2)}) collective-permute-start(f32[2,2,256,256]{3,2,1,0:T(8,128)} %copy-done.4), channel_id=1, source_target_pairs={{0,16},{16,32},{32,48},{48,64},{64,80},{80,96},{96,112},{112,128},... | collective-permute-start | bytes 3145736 | tf_op jit(solution)/shard_map/ppermute | solution.py:22
  68.0 0.6 copy-start.2
  68.6 15.1 %all-to-all-start.1 = ((f32[8,24,128]{2,1,0:T(8,128)}), f32[8,24,128]{2,1,0:T(8,128)S(1)}, u32[]{:S(2)}, u32[]{:S(2)}) async-start(f32[8,24,128]{2,1,0:T(8,128)} %copy-done.2), calls=%async_computation.1 | async-start | bytes 196608 | tf_op jit(solution)/shard_map/all_to_all | solution.py:296
  76.9 14.0 %collective-permute-start.7 = (f32[2,256,256]{2,1,0:T(8,128)}, f32[2,256,256]{2,1,0:T(8,128)S(1)}, u32[]{:S(2)}, u32[]{:S(2)}) collective-permute-start(f32[2,256,256]{2,1,0:T(8,128)} %fusion), channel_id=1, source_target_pairs={{0,1},{1,2},{2,3},{3,4},{4,5},{5,6},{6,7},{7,8},{8,9},{9,10},{10,1... | collective-permute-start | bytes 1572872 | tf_op jit(solution)/shard_map/ppermute | solution.py:22
  84.5 15.8 %all-to-all-start.2 = ((f32[32,16,128]{2,1,0:T(8,128)}), f32[32,16,128]{2,1,0:T(8,128)S(1)}, u32[]{:S(2)}, u32[]{:S(2)}) async-start(f32[32,16,128]{2,1,0:T(8,128)} %shard_map.71), calls=%async_computation.2 | async-start | bytes 524288 | tf_op jit(solution)/shard_map/all_to_all | solution.py:299
  100.3 7.0 %collective-permute-start.8 = (f32[32,16,128]{2,1,0:T(8,128)S(1)}, f32[32,16,128]{2,1,0:T(8,128)S(1)}, u32[]{:S(2)}, u32[]{:S(2)}) collective-permute-start(f32[32,16,128]{2,1,0:T(8,128)S(1)} %all-to-all-done.2), channel_id=1, source_target_pairs={{0,16},{16,0},{1,17},{17,1},{2,18},{18,2},{3,19},{19,3},{4,20},{20... | collective-permute-start | bytes 786440 | tf_op jit(solution)/shard_map/ppermute | solution.py:302

commit v6 on v5

--- a/solution.py
+++ b/solution.py
@@ -248,7 +248,7 @@
         out_shape=shape(count, *parts.shape[1:]),
         in_specs=[vmem()],
         out_specs=vmem(),
-        cost_estimate=pl.CostEstimate(flops=4000000000, bytes_accessed=1 << 19, transcendentals=0),
+        cost_estimate=pl.CostEstimate(flops=100000000000, bytes_accessed=1 << 19, transcendentals=0),
         compiler_params=pltpu.CompilerParams(vmem_limit_bytes=8 << 20),
     )(parts)
 
@@ -267,7 +267,7 @@
         out_shape=shape(count, 16, SIDE // 2),
         in_specs=[vmem(), vmem()],
         out_specs=vmem(),
-        cost_estimate=pl.CostEstimate(flops=100000, bytes_accessed=1 << 19, transcendentals=0),
+        cost_estimate=pl.CostEstimate(flops=100000000000, bytes_accessed=1 << 19, transcendentals=0),
         compiler_params=pltpu.CompilerParams(vmem_limit_bytes=8 << 20),
     )(parts, corner)
 

time: 109 us -> 109 us (level)
  no operation moved by 1% of the time
where the time goes in v6:
time: 109 us
  starting transfers between devices  66.2 us (61%)
  waiting for transfers between devices  26.3 us (24%)
  Pallas kernels  10.9 us (10%)
  other arithmetic  2.48 us (2%)
  local copies, waits for them, and re-layouts  1.98 us (2%)
    ppermute x7, starting transfers between devices, passed_along(): lax.ppermute(value, axis, [(source, source + steps) for source in range(l...  27.8 us
    all_to_all x1, starting transfers between devices, body(): summed = lax.all_to_all(pair, PLANE, 0, 0)  16.9 us
    all_to_all x1, starting transfers between devices, body(): summed = lax.all_to_all(fold(summed, lax.axis_size('y')), 'y', 0, 0)  7.44 us
    all_to_all x1, waiting for transfers between devices, body(): summed = lax.all_to_all(pair, PLANE, 0, 0)  7.38 us
    ppermute x7, waiting for transfers between devices, passed_along(): lax.ppermute(value, axis, [(source, source + steps) for source in range(l...  6.9 us
    all_to_all x1, waiting for transfers between devices, body(): near = lax.all_to_all(settle(summed, corner, rows), PLANE, 0, 0)  6.83 us
    ppermute x1, starting transfers between devices, body(): far = lax.ppermute(near, 'c', [(0, 1), (1, 0)])  6.09 us
    pallas_call x1, Pallas kernels, visit(): pl.pallas_call(visit_kernel, out_shape=out_shape, in_specs=[smem(), smem(...  6.04 us
  transfers between devices with their start and end apart: 12, of which 8 were waited for; matrix products, arithmetic and copies ran while one was open for 1% of the time, Pallas kernels for 4%

profile of v6, /device:TPU:1, one launch (start us, length us, event | category | flops | bytes accessed | tf_op | source)
XLA Modules:
  0.0 108.6 jit_solution(14117643560042168945)
XLA Ops:
  0.6 0.0 copy-start.2
  0.7 1.1 slice_bitcast_fusion.2
  1.7 1.3 %collective-permute-start = (f32[256,256]{1,0:T(8,128)S(1)}, f32[256,256]{1,0:T(8,128)S(1)}, u32[]{:S(2)}, u32[]{:S(2)}) collective-permute-start(f32[256,256]{1,0:T(8,128)S(1)} %slice_bitcast_fusion.2), channel_id=1, source_target_pairs={{1,0},{2,1},{3,2},{4,3},{5,4},{6,5},{7,6},{8,7},{9,8},{10,9},{11,1... | collective-permute-start | bytes 786440 | tf_op jit(solution)/shard_map/ppermute | solution.py:22
  3.0 1.3 %collective-permute-start.1 = (f32[256,256]{1,0:T(8,128)S(1)}, f32[256,256]{1,0:T(8,128)S(1)}, u32[]{:S(2)}, u32[]{:S(2)}) collective-permute-start(f32[256,256]{1,0:T(8,128)S(1)} %slice_bitcast_fusion.1), channel_id=1, source_target_pairs={{1,0},{2,1},{3,2},{4,3},{5,4},{6,5},{7,6},{8,7},{9,8},{10,9},{11,1... | collective-permute-start | bytes 786440 | tf_op jit(solution)/shard_map/ppermute | solution.py:22
  4.3 8.8 %collective-permute-start.2 = (f32[2,256,256]{2,1,0:T(8,128)S(1)}, f32[2,256,256]{2,1,0:T(8,128)S(1)}, u32[]{:S(2)}, u32[]{:S(2)}) collective-permute-start(f32[2,256,256]{2,1,0:T(8,128)S(1)} %copy-done.2), channel_id=1, source_target_pairs={{16,0},{32,16},{48,32},{64,48},{80,64},{96,80},{112,96},{128,112},... | collective-permute-start | bytes 1572872 | tf_op jit(solution)/shard_map/ppermute | solution.py:22
  13.2 0.7 copy-done.4
  13.8 0.9 shard_map.68.rolled_probe
  14.8 3.9 %collective-permute-start.3 = (f32[256,256]{1,0:T(8,128)S(1)}, f32[256,256]{1,0:T(8,128)S(1)}, u32[]{:S(2)}, u32[]{:S(2)}) collective-permute-start(f32[256,256]{1,0:T(8,128)S(1)} %collective-permute-done.right_real), channel_id=1, source_target_pairs={{16,0},{32,16},{48,32},{64,48},{80,64},{96,80},{112,96},{128,112},... | collective-permute-start | bytes 786440 | tf_op jit(solution)/shard_map/ppermute | solution.py:22
  18.8 2.8 %collective-permute-start.4 = (f32[256,256]{1,0:T(8,128)S(1)}, f32[256,256]{1,0:T(8,128)S(1)}, u32[]{:S(2)}, u32[]{:S(2)}) collective-permute-start(f32[256,256]{1,0:T(8,128)S(1)} %collective-permute-done.1.right_imag), channel_id=1, source_target_pairs={{16,0},{32,16},{48,32},{64,48},{80,64},{96,80},{112,96},{128,112},... | collective-permute-start | bytes 786440 | tf_op jit(solution)/shard_map/ppermute | solution.py:22
  21.6 2.5 %collective-permute-done.3.corner_real = f32[256,256]{1,0:T(8,128)S(1)} collective-permute-done((f32[256,256]{1,0:T(8,128)S(1)}, f32[256,256]{1,0:T(8,128)S(1)}, u32[]{:S(2)}, u32[]{:S(2)}) %collective-permute-start.3) | collective-permute-done | bytes 262176 | tf_op jit(solution)/shard_map/ppermute | solution.py:22
  24.0 4.0 %collective-permute-done.4.corner_imag = f32[256,256]{1,0:T(8,128)S(1)} collective-permute-done((f32[256,256]{1,0:T(8,128)S(1)}, f32[256,256]{1,0:T(8,128)S(1)}, u32[]{:S(2)}, u32[]{:S(2)}) %collective-permute-start.4) | collective-permute-done | bytes 262176 | tf_op jit(solution)/shard_map/ppermute | solution.py:22
  28.0 6.0 %shard_map.69 = (f32[32,3,8,128]{3,2,1,0:T(8,128)S(1)}, f32[32,3,8,128]{3,2,1,0:T(8,128)S(1)}, f32[2,256,256]{2,1,0:T(8,128)S(1)}, f32[2,256,256]{2,1,0:T(8,128)S(1)}, f32[2,2,256,256]{3,2,1,0:T(8,128)S(1)}) custom-call(s32[2,2]{1,0:T(2,128)S(1)} %bitcast.21, s32[1]{0:T(128)} %bitcast.1.core, f32[2,256,256]{2,1,0:T(8,128)S(1)} %copy-done.2, ...), custom_call_target="tpu_custom_call" | custom-call | flops 3221225472 | bytes 8388608 | tf_op jit(solution)/shard_map/pallas_call | solution.py:228
  34.1 1.9 %collective-permute-start.5 = (f32[32,3,8,128]{3,2,1,0:T(8,128)S(1)}, f32[32,3,8,128]{3,2,1,0:T(8,128)S(1)}, u32[]{:S(2)}, u32[]{:S(2)}) collective-permute-start(f32[32,3,8,128]{3,2,1,0:T(8,128)S(1)} %get-tuple-element.19), channel_id=1, source_target_pairs={{0,16},{16,0},{1,17},{17,1},{2,18},{18,2},{3,19},{19,3},{4,20},{20... | collective-permute-start | bytes 1179656 | tf_op jit(solution)/shard_map/ppermute | solution.py:290
  36.0 1.7 %collective-permute-done.5 = f32[32,3,8,128]{3,2,1,0:T(8,128)S(1)} collective-permute-done((f32[32,3,8,128]{3,2,1,0:T(8,128)S(1)}, f32[32,3,8,128]{3,2,1,0:T(8,128)S(1)}, u32[]{:S(2)}, u32[]{:S(2)}) %collective-permute-start.5) | collective-permute-done | bytes 393248 | tf_op jit(solution)/shard_map/ppermute | solution.py:290
  37.7 0.8 add_bitcast_fusion
  38.5 16.9 %all-to-all-start = ((f32[32,24,128]{2,1,0:T(8,128)}), f32[32,24,128]{2,1,0:T(8,128)S(1)}, u32[]{:S(2)}, u32[]{:S(2)}) async-start(f32[32,24,128]{2,1,0:T(8,128)} %add_bitcast_fusion), calls=%async_computation | async-start | bytes 786432 | tf_op jit(solution)/shard_map/all_to_all | solution.py:294
  55.4 5.2 %collective-permute-start.6 = (f32[2,2,256,256]{3,2,1,0:T(8,128)}, f32[2,2,256,256]{3,2,1,0:T(8,128)S(1)}, u32[]{:S(2)}, u32[]{:S(2)}) collective-permute-start(f32[2,2,256,256]{3,2,1,0:T(8,128)} %copy-done.6), channel_id=1, source_target_pairs={{0,16},{16,32},{32,48},{48,64},{64,80},{80,96},{96,112},{112,128},... | collective-permute-start | bytes 3145736 | tf_op jit(solution)/shard_map/ppermute | solution.py:22
  60.7 7.4 %all-to-all-done.parts = f32[32,24,128]{2,1,0:T(8,128)S(1)} async-done(((f32[32,24,128]{2,1,0:T(8,128)}), f32[32,24,128]{2,1,0:T(8,128)S(1)}, u32[]{:S(2)}, u32[]{:S(2)}) %all-to-all-start) | async-done | bytes 393248 | tf_op jit(solution)/shard_map/all_to_all | solution.py:294
  68.0 0.7 shard_map.70
  68.7 7.4 %all-to-all-start.1 = ((f32[8,24,128]{2,1,0:T(8,128)}), f32[8,24,128]{2,1,0:T(8,128)S(1)}, u32[]{:S(2)}, u32[]{:S(2)}) async-start(f32[8,24,128]{2,1,0:T(8,128)} %shard_map.70), calls=%async_computation.1 | async-start | bytes 196608 | tf_op jit(solution)/shard_map/all_to_all | solution.py:296
  76.2 0.9 fusion
  77.0 4.5 %collective-permute-start.7 = (f32[2,256,256]{2,1,0:T(8,128)}, f32[2,256,256]{2,1,0:T(8,128)S(1)}, u32[]{:S(2)}, u32[]{:S(2)}) collective-permute-start(f32[2,256,256]{2,1,0:T(8,128)} %fusion), channel_id=1, source_target_pairs={{0,1},{1,2},{2,3},{3,4},{4,5},{5,6},{6,7},{7,8},{8,9},{9,10},{10,1... | collective-permute-start | bytes 1572872 | tf_op jit(solution)/shard_map/ppermute | solution.py:22
  81.5 2.3 %all-to-all-done.1.parts = f32[8,24,128]{2,1,0:T(8,128)S(1)} async-done(((f32[8,24,128]{2,1,0:T(8,128)}), f32[8,24,128]{2,1,0:T(8,128)S(1)}, u32[]{:S(2)}, u32[]{:S(2)}) %all-to-all-start.1) | async-done | bytes 98336 | tf_op jit(solution)/shard_map/all_to_all | solution.py:296
  83.9 0.7 shard_map.71
  84.6 6.0 %all-to-all-start.2 = ((f32[32,16,128]{2,1,0:T(8,128)}), f32[32,16,128]{2,1,0:T(8,128)S(1)}, u32[]{:S(2)}, u32[]{:S(2)}) async-start(f32[32,16,128]{2,1,0:T(8,128)} %shard_map.71), calls=%async_computation.2 | async-start | bytes 524288 | tf_op jit(solution)/shard_map/all_to_all | solution.py:299
  90.6 0.5 collective-permute-done.7.step_right
  91.1 0.2 copy-done.5
  91.2 2.5 %shard_map.72 = f32[2,256,256]{2,1,0:T(8,128)} custom-call(s32[2,2]{1,0:T(2,128)S(1)} %bitcast.22, f32[2,256,256]{2,1,0:T(8,128)S(1)} %copy-done.1, f32[2,256,256]{2,1,0:T(8,128)S(1)} %copy-done.3, f32[2,256,256]{2,1,0:T(8,128)S(1)} %get-tuple-element.25.step_own, f32[2,2,256,256]{3,2,1,0:T(8,128)S(1)} %collective-permute-done.6.step_row, ...), custom_call_target="tpu_custom_call" | custom-call | flops 8000000 | bytes 8388608 | tf_op jit(solution)/shard_map/pallas_call | solution.py:209
  93.7 6.8 %all-to-all-done.2 = f32[32,16,128]{2,1,0:T(8,128)S(1)} async-done(((f32[32,16,128]{2,1,0:T(8,128)}), f32[32,16,128]{2,1,0:T(8,128)S(1)}, u32[]{:S(2)}, u32[]{:S(2)}) %all-to-all-start.2) | async-done | bytes 262176 | tf_op jit(solution)/shard_map/all_to_all | solution.py:299
  100.6 6.1 %collective-permute-start.8 = (f32[32,16,128]{2,1,0:T(8,128)S(1)}, f32[32,16,128]{2,1,0:T(8,128)S(1)}, u32[]{:S(2)}, u32[]{:S(2)}) collective-permute-start(f32[32,16,128]{2,1,0:T(8,128)S(1)} %all-to-all-done.2), channel_id=1, source_target_pairs={{0,16},{16,0},{1,17},{17,1},{2,18},{18,2},{3,19},{19,3},{4,20},{20... | collective-permute-start | bytes 786440 | tf_op jit(solution)/shard_map/ppermute | solution.py:302
  106.7 1.1 %collective-permute-done.8 = f32[32,16,128]{2,1,0:T(8,128)S(1)} collective-permute-done((f32[32,16,128]{2,1,0:T(8,128)S(1)}, f32[32,16,128]{2,1,0:T(8,128)S(1)}, u32[]{:S(2)}, u32[]{:S(2)}) %collective-permute-start.8) | collective-permute-done | bytes 262176 | tf_op jit(solution)/shard_map/ppermute | solution.py:302
  107.8 0.8 copy_bitcast_fusion
  (21 shorter events, 0.1 us)
Async XLA Ops:
  0.6 2.4 %copy-start.2 = (f32[2,256,256]{2,1,0:T(8,128)S(1)}, f32[2,256,256]{2,1,0:T(8,128)}, u32[]{:S(2)}) copy-start(f32[2,256,256]{2,1,0:T(8,128)} %tile.3) | copy-start | bytes 1572868
  0.6 12.5 %copy-start = (f32[2,256,256]{2,1,0:T(8,128)S(1)}, f32[2,256,256]{2,1,0:T(8,128)}, u32[]{:S(2)}) copy-start(f32[2,256,256]{2,1,0:T(8,128)} %probe.3) | copy-start | bytes 1572868
  1.7 13.1 %collective-permute-start = (f32[256,256]{1,0:T(8,128)S(1)}, f32[256,256]{1,0:T(8,128)S(1)}, u32[]{:S(2)}, u32[]{:S(2)}) collective-permute-start(f32[256,256]{1,0:T(8,128)S(1)} %slice_bitcast_fusion.2), channel_id=1, source_target_pairs={{1,0},{2,1},{3,2},{4,3},{5,4},{6,5},{7,6},{8,7},{9,8},{10,9},{11,1... | collective-permute-start | bytes 786440 | tf_op jit(solution)/shard_map/ppermute | solution.py:22
  3.0 15.7 %collective-permute-start.1 = (f32[256,256]{1,0:T(8,128)S(1)}, f32[256,256]{1,0:T(8,128)S(1)}, u32[]{:S(2)}, u32[]{:S(2)}) collective-permute-start(f32[256,256]{1,0:T(8,128)S(1)} %slice_bitcast_fusion.1), channel_id=1, source_target_pairs={{1,0},{2,1},{3,2},{4,3},{5,4},{6,5},{7,6},{8,7},{9,8},{10,9},{11,1... | collective-permute-start | bytes 786440 | tf_op jit(solution)/shard_map/ppermute | solution.py:22
  4.3 23.6 %collective-permute-start.2 = (f32[2,256,256]{2,1,0:T(8,128)S(1)}, f32[2,256,256]{2,1,0:T(8,128)S(1)}, u32[]{:S(2)}, u32[]{:S(2)}) collective-permute-start(f32[2,256,256]{2,1,0:T(8,128)S(1)} %copy-done.2), channel_id=1, source_target_pairs={{16,0},{32,16},{48,32},{64,48},{80,64},{96,80},{112,96},{128,112},... | collective-permute-start | bytes 1572872 | tf_op jit(solution)/shard_map/ppermute | solution.py:22
  13.2 0.7 copy-start.4
  13.8 14.2 %copy-start.7 = (bf16[1,1,2,256,256]{4,3,2,1,0:T(8,128)(2,1)S(1)}, bf16[1,1,2,256,256]{4,3,2,1,0:T(8,128)(2,1)}, u32[]{:S(2)}) copy-start(bf16[1,1,2,256,256]{4,3,2,1,0:T(8,128)(2,1)} %param.6) | copy-start | bytes 786436
  13.8 14.2 %copy-start.8 = (bf16[3,2,256,256]{3,2,1,0:T(8,128)(2,1)S(1)}, bf16[3,2,256,256]{3,2,1,0:T(8,128)(2,1)}, u32[]{:S(2)}) copy-start(bf16[3,2,256,256]{3,2,1,0:T(8,128)(2,1)} %constant.29.clone.tables) | copy-start | bytes 2359300
  14.8 9.2 %collective-permute-start.3 = (f32[256,256]{1,0:T(8,128)S(1)}, f32[256,256]{1,0:T(8,128)S(1)}, u32[]{:S(2)}, u32[]{:S(2)}) collective-permute-start(f32[256,256]{1,0:T(8,128)S(1)} %collective-permute-done.right_real), channel_id=1, source_target_pairs={{16,0},{32,16},{48,32},{64,48},{80,64},{96,80},{112,96},{128,112},... | collective-permute-start | bytes 786440 | tf_op jit(solution)/shard_map/ppermute | solution.py:22
  18.8 9.2 %collective-permute-start.4 = (f32[256,256]{1,0:T(8,128)S(1)}, f32[256,256]{1,0:T(8,128)S(1)}, u32[]{:S(2)}, u32[]{:S(2)}) collective-permute-start(f32[256,256]{1,0:T(8,128)S(1)} %collective-permute-done.1.right_imag), channel_id=1, source_target_pairs={{16,0},{32,16},{48,32},{64,48},{80,64},{96,80},{112,96},{128,112},... | collective-permute-start | bytes 786440 | tf_op jit(solution)/shard_map/ppermute | solution.py:22
  34.0 4.4 %copy-start.6 = (f32[2,2,256,256]{3,2,1,0:T(8,128)}, f32[2,2,256,256]{3,2,1,0:T(8,128)S(1)}, u32[]{:S(2)}) copy-start(f32[2,2,256,256]{3,2,1,0:T(8,128)S(1)} %get-tuple-element.22) | copy-start | bytes 3145732
  34.1 3.6 %collective-permute-start.5 = (f32[32,3,8,128]{3,2,1,0:T(8,128)S(1)}, f32[32,3,8,128]{3,2,1,0:T(8,128)S(1)}, u32[]{:S(2)}, u32[]{:S(2)}) collective-permute-start(f32[32,3,8,128]{3,2,1,0:T(8,128)S(1)} %get-tuple-element.19), channel_id=1, source_target_pairs={{0,16},{16,0},{1,17},{17,1},{2,18},{18,2},{3,19},{19,3},{4,20},{20... | collective-permute-start | bytes 1179656 | tf_op jit(solution)/shard_map/ppermute | solution.py:290
  38.5 29.6 %all-to-all-start = ((f32[32,24,128]{2,1,0:T(8,128)}), f32[32,24,128]{2,1,0:T(8,128)S(1)}, u32[]{:S(2)}, u32[]{:S(2)}) async-start(f32[32,24,128]{2,1,0:T(8,128)} %add_bitcast_fusion), calls=%async_computation | async-start | bytes 786432 | tf_op jit(solution)/shard_map/all_to_all | solution.py:294
  55.4 20.8 %collective-permute-start.6 = (f32[2,2,256,256]{3,2,1,0:T(8,128)}, f32[2,2,256,256]{3,2,1,0:T(8,128)S(1)}, u32[]{:S(2)}, u32[]{:S(2)}) collective-permute-start(f32[2,2,256,256]{3,2,1,0:T(8,128)} %copy-done.6), channel_id=1, source_target_pairs={{0,16},{16,32},{32,48},{48,64},{64,80},{80,96},{96,112},{112,128},... | collective-permute-start | bytes 3145736 | tf_op jit(solution)/shard_map/ppermute | solution.py:22
  68.7 15.1 %all-to-all-start.1 = ((f32[8,24,128]{2,1,0:T(8,128)}), f32[8,24,128]{2,1,0:T(8,128)S(1)}, u32[]{:S(2)}, u32[]{:S(2)}) async-start(f32[8,24,128]{2,1,0:T(8,128)} %shard_map.70), calls=%async_computation.1 | async-start | bytes 196608 | tf_op jit(solution)/shard_map/all_to_all | solution.py:296
  77.0 14.0 %collective-permute-start.7 = (f32[2,256,256]{2,1,0:T(8,128)}, f32[2,256,256]{2,1,0:T(8,128)S(1)}, u32[]{:S(2)}, u32[]{:S(2)}) collective-permute-start(f32[2,256,256]{2,1,0:T(8,128)} %fusion), channel_id=1, source_target_pairs={{0,1},{1,2},{2,3},{3,4},{4,5},{5,6},{6,7},{7,8},{8,9},{9,10},{10,1... | collective-permute-start | bytes 1572872 | tf_op jit(solution)/shard_map/ppermute | solution.py:22
  83.8 7.2 %copy-start.3 = (f32[2,256,256]{2,1,0:T(8,128)S(1)}, f32[2,256,256]{2,1,0:T(8,128)}, u32[]{:S(2)}) copy-start(f32[2,256,256]{2,1,0:T(8,128)} %tile.3) | copy-start | bytes 1572868
  84.6 6.5 %copy-start.1 = (f32[2,256,256]{2,1,0:T(8,128)S(1)}, f32[2,256,256]{2,1,0:T(8,128)}, u32[]{:S(2)}) copy-start(f32[2,256,256]{2,1,0:T(8,128)} %probe.3) | copy-start | bytes 1572868
  84.6 16.0 %all-to-all-start.2 = ((f32[32,16,128]{2,1,0:T(8,128)}), f32[32,16,128]{2,1,0:T(8,128)S(1)}, u32[]{:S(2)}, u32[]{:S(2)}) async-start(f32[32,16,128]{2,1,0:T(8,128)} %shard_map.71), calls=%async_computation.2 | async-start | bytes 524288 | tf_op jit(solution)/shard_map/all_to_all | solution.py:299
  90.6 0.7 copy-start.5
  100.6 7.2 %collective-permute-start.8 = (f32[32,16,128]{2,1,0:T(8,128)S(1)}, f32[32,16,128]{2,1,0:T(8,128)S(1)}, u32[]{:S(2)}, u32[]{:S(2)}) collective-permute-start(f32[32,16,128]{2,1,0:T(8,128)S(1)} %all-to-all-done.2), channel_id=1, source_target_pairs={{0,16},{16,0},{1,17},{17,1},{2,18},{18,2},{3,19},{19,3},{4,20},{20... | collective-permute-start | bytes 786440 | tf_op jit(solution)/shard_map/ppermute | solution.py:302
